TPU v7x, 32 devices: a whole 2x2x4 slice. The times are simulated.
32 devices in a mesh: row: 4 (over x, core), col: 8 (over z, y).
Axes of the slice: x: 2, y: 2, z: 4, core: 2. Of those that a mesh axis runs over, the one named last changes fastest.
Arguments:
- volt_init: float32 [32, 128, 400], P('row', 'col'), may hold values from -6 to 6
- curr_init: float32 [32, 128, 400], P('row', 'col'), may hold values from -6 to 6
- local_inverse: bfloat16 [32, 400, 400], P('row'), may hold values from -1 to 2, as said below
- schur_inverse: bfloat16 [4096, 4096], P('row', 'col'), may hold values from -1 to 2, as said below
- ind_gain: float32 [32, 400], P('row'), may hold values from 0.05 to 0.5
- tie: float32 [32, 64], P('row'), may hold values from 0.3 to 3
- port_map: int32 [32, 64], P('row'), may hold values from 0 to 4095
- breaker: int32 [32, 128, 400], P('row', 'col'), may hold values 0 or 1
- fault_time: int32 [128], P('col'), may hold values from 0 to 2
- fault_node: int32 [128], P('col'), may hold values from 0 to 12799
Outputs:
- volt_final: float32 [32, 128, 400], P('row', 'col')
- curr_final: float32 [32, 128, 400], P('row', 'col')
- iface_volt: float32 [128, 4096], P('col', 'row')
Inputs may be any that keep to these rules, and one draw needn't show every extreme that they name: `local_inverse`: diagonal entries between 0.5 and 1.5; off-diagonal entries independent. `schur_inverse`: diagonal entries between 0.5 and 1.5; off-diagonal entries independent.
All inputs are finite; a program needn't handle non-finite values. No bound on the sum of `breaker` on one device may be relied on, other than what follows from the above.
Results may differ from a plain program's by a relative error of at most 0.0068.
Values may be sent and summed in bfloat16 or wider, within the bound.
A program may use at most 64 MiB of HBM per device.

v0:
```python
import jax
import jax.numpy as jnp
from jax import lax
from jax.sharding import PartitionSpec as P

STEPS = 2


def local(
    volt_init,
    curr_init,
    local_inverse,
    schur_inverse,
    ind_gain,
    tie,
    port_map,
    breaker,
    fault_time,
    fault_node,
):
    sub_count, scen_count, node_count = volt_init.shape
    port_count = tie.shape[1]
    iface_width = lax.axis_size("row") * schur_inverse.shape[0]
    volt = volt_init
    curr = curr_init
    closed = breaker.astype(jnp.float32)
    first_sub = lax.axis_index("row") * sub_count
    node_ids = (first_sub + jnp.arange(sub_count, dtype=jnp.int32))[
        :, None
    ] * node_count + jnp.arange(node_count, dtype=jnp.int32)[None, :]
    hits = node_ids[:, None, :] == fault_node[None, :, None]
    flat_map = port_map.reshape(-1)
    port_inverse = local_inverse[:, :port_count, :]
    iface_block = jnp.zeros((scen_count, schur_inverse.shape[0]), jnp.float32)
    for step in range(STEPS):
        hist = closed * (curr + ind_gain[:, None, :] * volt)
        active = (step >= fault_time)[None, :, None]
        fault_on = jnp.where(hits & active, 1.0, 0.0).astype(jnp.float32)
        inject = (-hist - 2.0 * fault_on * volt).astype(jnp.bfloat16)
        open_volt = jnp.einsum(
            "ksn,knm->ksm", inject, local_inverse, preferred_element_type=jnp.float32
        )
        values = tie[:, None, :] * open_volt[:, :, :port_count]
        flat_values = jnp.transpose(values, (0, 2, 1)).reshape(sub_count * port_count, scen_count)
        partial_rhs = jax.ops.segment_sum(flat_values, flat_map, iface_width).T
        owned = lax.psum_scatter(partial_rhs, "row", scatter_dimension=1, tiled=True)
        rhs_half = lax.all_gather(owned.astype(jnp.bfloat16), "row", axis=1, tiled=True)
        iface_block = lax.dot_general(
            rhs_half,
            lax.all_gather(schur_inverse, "col", axis=1, tiled=True),
            (((1,), (1,)), ((), ())),
            preferred_element_type=jnp.float32,
        )
        iface_full = lax.all_gather(iface_block, "row", axis=1, tiled=True)
        picked = jnp.take(iface_full, flat_map, axis=1).reshape(scen_count, sub_count, port_count)
        drive = (tie[:, None, :] * jnp.transpose(picked, (1, 0, 2))).astype(jnp.bfloat16)
        volt_next = open_volt + jnp.einsum(
            "ksp,kpn->ksn", drive, port_inverse, preferred_element_type=jnp.float32
        )
        curr = closed * (curr + ind_gain[:, None, :] * (volt_next + volt))
        volt = volt_next
    return (volt, curr, iface_block)


def solution(mesh):
    placed = (
        P("row", "col", None),
        P("row", "col", None),
        P("row", None, None),
        P("row", "col"),
        P("row", None),
        P("row", None),
        P("row", None),
        P("row", "col", None),
        P("col"),
        P("col"),
    )
    return jax.shard_map(
        local,
        mesh=mesh,
        in_specs=placed,
        out_specs=(P("row", "col", None), P("row", "col", None), P("col", "row")),
        check_vma=False,
    )
```

profile of v0, /device:TPU:0, one launch (start us, length us, event | category | flops | bytes accessed | tf_op | source)
XLA Modules:
  0.0 253.1 jit_solution(16327846174430258213)
XLA Ops:
  8.0 0.0 copy-start.8
  8.0 0.0 reduce-scatter.3.cloned.1.call-start
  8.1 1.2 broadcast_compare_fusion
  9.3 0.8 reshape.77
  10.1 0.0 copy-start.10
  10.1 0.1 iota_add_fusion
  10.1 0.0 copy-start.7
  10.1 2.8 %fusion.6 = f32[8,16,400]{2,1,0:T(8,128)S(1)} fusion(bf16[8,400,400]{2,1,0:T(8,128)(2,1)} %param.14, f32[8,16,400]{2,1,0:T(8,128)} %param.12, f32[8,16,400]{2,1,0:T(8,128)} %param.13, s32[8,16,400]{2,1,0:T(8,128)} %param.19, s32[8,400]{1,0:T(8,128)S(1)} %iota_add_fusion, f32[8,400]{1,0:T(8,128)} %param.16, s32[16]{0:T(128)} %param.21, ...), kind=kOutput, calls=%fused_computation.18 | convolution fusion | flops 41574400 | bytes 3404880 | tf_op jit(solution)/shard_map/ksn,knm->ksm/dot_general | solution.py:40
  12.9 0.0 copy-done.7
  12.9 0.0 copy-start.3
  13.0 0.7 copy-done.3
  13.7 0.0 copy-done.8
  13.7 0.1 copy.31
  13.8 3.7 %scatter_custom_fusion = f32[4096,16]{1,0:T(8,128)} fusion(s32[512]{0:T(512)S(1)} %reshape.77, f32[512,16]{1,0:T(8,128)S(1)} %bitcast.33, f32[]{:T(128)} %constant.7.clone.1), kind=kCustom, calls=%fused_computation.8 | custom fusion | flops 8192 | bytes 262148 | tf_op jit(solution)/shard_map/scatter-add | solution.py:45
  17.5 0.0 reduce-scatter.3.cloned.1.call-update
  17.5 0.0 all-gather.2.cloned.1.call-start
  17.6 0.5 all-gather.2.cloned.1.call-update
  18.1 0.0 reduce-scatter.5.cloned.1.call-start
  18.2 0.6 pad_clamp_fusion
  18.8 0.0 copy-done.10
  18.8 0.6 compare_and_fusion.2
  19.3 32.5 %reduce-scatter.3.cloned.1.call-done = f32[16,1024]{0,1:T(8,128)} async-done(((f32[16,4096]{0,1:T(8,128)}), f32[16,1024]{0,1:T(8,128)}) %reduce-scatter.3.cloned.1.call-update) | async-done | bytes 65552 | tf_op jit(solution)/shard_map/reduce_scatter | solution.py:46
  51.8 1.1 convert_element_type.29
  52.9 9.6 %all_gather.16 = bf16[16,4096]{0,1:T(8,128)(2,1)S(1)} all-gather(bf16[16,1024]{0,1:T(8,128)(2,1)S(1)} %convert_element_type.29), channel_id=1, replica_groups=mesh['row'=4,'col'=8] {'row'}, dimensions={1}, use_global_device_ids=true | all-gather | bytes 163840 | tf_op jit(solution)/shard_map/all_gather | solution.py:47
  62.5 85.5 %all-gather.2.cloned.1.call-done = bf16[1024,4096]{1,0:T(8,128)(2,1)} async-done(((bf16[1024,512]{1,0:T(8,128)(2,1)}), bf16[1024,4096]{1,0:T(8,128)(2,1)}) %all-gather.2.cloned.1.call-update) | async-done | bytes 8388624 | tf_op jit(solution)/shard_map/all_gather | solution.py:50
  148.0 5.6 %fusion.36 = f32[16,1024]{1,0:T(8,128)S(1)} fusion(bf16[16,4096]{0,1:T(8,128)(2,1)S(1)} %all_gather.16, bf16[1024,4096]{1,0:T(8,128)(2,1)} %all-gather.2.cloned.1.call-done), kind=kOutput, calls=%fused_computation.59 | convolution fusion | flops 134217728 | bytes 8585216 | tf_op jit(solution)/shard_map/dot_general | solution.py:48
  153.6 0.0 copy-start
  153.6 0.0 copy-start.1
  153.6 0.0 copy-start.6
  153.6 6.4 %all_gather.18 = f32[16,4096]{1,0:T(8,128)} all-gather(f32[16,1024]{1,0:T(8,128)S(1)} %fusion.36), channel_id=1, replica_groups=mesh['row'=4,'col'=8] {'row'}, dimensions={1}, use_global_device_ids=true | all-gather | bytes 327680 | tf_op jit(solution)/shard_map/all_gather | solution.py:54
  160.0 2.9 %copy.25 = f32[16,4096]{0,1:T(8,128)} copy(f32[16,4096]{1,0:T(8,128)} %all_gather.18) | data formatting | bytes 524288 | tf_op jit(solution)/shard_map/all_gather | solution.py:54
  163.0 3.4 %gather_fusion = f32[512,16]{1,0:T(8,128)} fusion(f32[16,4096]{0,1:T(8,128)} %copy.25, s32[1024]{0:T(1024)} %pad_clamp_fusion), kind=kCustom, calls=%fused_computation.clone | custom fusion | bytes 67584 | tf_op jit(solution)/shard_map/jit(_take)/gather | solution.py:55
  166.3 1.8 broadcast_select_fusion.1
  168.1 1.7 copy.26
  169.8 0.0 copy-done
  169.8 0.0 copy-start.9
  169.8 1.2 convolution_add_fusion.1
  171.0 0.0 copy-start.2
  171.0 0.7 copy-done.2
  171.7 0.0 copy-done.1
  171.7 0.0 copy-done.6
  171.7 1.6 fusion.7
  173.4 0.0 copy-start.4
  173.4 0.7 copy-done.4
  174.1 0.0 copy-done.9
  174.1 0.6 fusion.22
  174.7 1.7 copy.32
  176.4 4.1 %scatter_custom_fusion.1 = f32[4096,16]{1,0:T(8,128)} fusion(s32[512]{0:T(512)} %copy-done.10, f32[512,16]{1,0:T(8,128)} %bitcast.32, f32[]{:T(128)} %constant.7.clone.1), kind=kCustom, calls=%fused_computation.6 | custom fusion | flops 8192 | bytes 262656 | tf_op jit(solution)/shard_map/scatter-add | solution.py:45
  180.5 0.0 reduce-scatter.5.cloned.1.call-update
  180.5 29.8 %reduce-scatter.5.cloned.1.call-done = f32[16,1024]{0,1:T(8,128)} async-done(((f32[16,4096]{0,1:T(8,128)}), f32[16,1024]{0,1:T(8,128)}) %reduce-scatter.5.cloned.1.call-update) | async-done | bytes 65552 | tf_op jit(solution)/shard_map/reduce_scatter | solution.py:46
  210.3 1.1 convert_element_type.33
  211.4 9.6 %all_gather.19 = bf16[16,4096]{0,1:T(8,128)(2,1)S(1)} all-gather(bf16[16,1024]{0,1:T(8,128)(2,1)S(1)} %convert_element_type.33), channel_id=1, replica_groups=mesh['row'=4,'col'=8] {'row'}, dimensions={1}, use_global_device_ids=true | all-gather | bytes 163840 | tf_op jit(solution)/shard_map/all_gather | solution.py:47
  221.0 5.7 %fusion.37 = f32[16,1024]{1,0:T(8,128)S(1)} fusion(bf16[16,4096]{0,1:T(8,128)(2,1)S(1)} %all_gather.19, bf16[1024,4096]{1,0:T(8,128)(2,1)} %all-gather.2.cloned.1.call-done), kind=kOutput, calls=%fused_computation.60 | convolution fusion | flops 134217728 | bytes 8585216 | tf_op jit(solution)/shard_map/dot_general | solution.py:48
  226.7 0.0 copy-start.5
  226.7 0.6 copy-done.5
  227.3 6.3 %all_gather.20 = f32[16,4096]{1,0:T(8,128)} all-gather(f32[16,1024]{1,0:T(8,128)S(1)} %fusion.37), channel_id=1, replica_groups=mesh['row'=4,'col'=8] {'row'}, dimensions={1}, use_global_device_ids=true | all-gather | bytes 327680 | tf_op jit(solution)/shard_map/all_gather | solution.py:54
  233.7 2.9 %copy.29 = f32[16,4096]{0,1:T(8,128)} copy(f32[16,4096]{1,0:T(8,128)} %all_gather.20) | data formatting | bytes 524288 | tf_op jit(solution)/shard_map/all_gather | solution.py:54
  236.6 3.4 %gather_fusion.1 = f32[512,16]{1,0:T(8,128)} fusion(f32[16,4096]{0,1:T(8,128)} %copy.29, s32[1024]{0:T(1024)} %pad_clamp_fusion), kind=kCustom, calls=%fused_computation.1.clone | custom fusion | bytes 67584 | tf_op jit(solution)/shard_map/jit(_take)/gather | solution.py:55
  239.9 1.8 broadcast_select_fusion
  241.7 1.7 copy.30
  243.4 2.2 add_multiply_fusion
  (3 shorter events, 0.0 us)
Async XLA Ops:
  8.0 5.7 %copy-start.8 = (f32[8,64]{1,0:T(8,128)S(1)}, f32[8,64]{1,0:T(8,128)}, u32[]{:S(2)}) copy-start(f32[8,64]{1,0:T(8,128)} %param.17) | copy-start | bytes 6148
  8.0 43.8 %reduce-scatter.3.cloned.1.call-start = ((), (), s32[]{:S(2)}) async-start(), calls=%async_computation.2 | async-start | bytes 2621440 | tf_op jit(solution)/shard_map/reduce_scatter | solution.py:46
  10.1 8.7 %copy-start.10 = (s32[512]{0:T(512)}, s32[512]{0:T(512)S(1)}, u32[]{:S(2)}) copy-start(s32[512]{0:T(512)S(1)} %reshape.77) | copy-start | bytes 6148
  10.1 2.8 %copy-start.7 = (s32[8,400]{1,0:T(8,128)}, s32[8,400]{1,0:T(8,128)S(1)}, u32[]{:S(2)}) copy-start(s32[8,400]{1,0:T(8,128)S(1)} %iota_add_fusion) | copy-start | bytes 38404
  12.9 0.7 copy-start.3
  17.5 130.4 %all-gather.2.cloned.1.call-start = ((), (), s32[]{:S(2)}) async-start(), calls=%async_computation.3 | async-start | bytes 9437184 | tf_op jit(solution)/shard_map/all_gather | solution.py:50
  18.1 192.2 %reduce-scatter.5.cloned.1.call-start = ((), (), s32[]{:S(2)}) async-start(), calls=%async_computation.4 | async-start | bytes 2621440 | tf_op jit(solution)/shard_map/reduce_scatter | solution.py:46
  153.6 16.2 %copy-start = (bf16[8,400,400]{2,1,0:T(8,128)(2,1)S(1)}, bf16[8,400,400]{2,1,0:T(8,128)(2,1)}, u32[]{:S(2)}) copy-start(bf16[8,400,400]{2,1,0:T(8,128)(2,1)} %param.14) | copy-start | bytes 7680004
  153.6 18.1 %copy-start.1 = (f32[8,16,400]{2,1,0:T(8,128)S(1)}, f32[8,16,400]{2,1,0:T(8,128)}, u32[]{:S(2)}) copy-start(f32[8,16,400]{2,1,0:T(8,128)} %param.12) | copy-start | bytes 614404
  153.6 18.1 %copy-start.6 = (f32[8,400]{1,0:T(8,128)S(1)}, f32[8,400]{1,0:T(8,128)}, u32[]{:S(2)}) copy-start(f32[8,400]{1,0:T(8,128)} %param.16) | copy-start | bytes 38404
  169.8 4.3 %copy-start.9 = (f32[8,64]{1,0:T(8,128)S(1)}, f32[8,64]{1,0:T(8,128)}, u32[]{:S(2)}) copy-start(f32[8,64]{1,0:T(8,128)} %param.17) | copy-start | bytes 6148
  171.0 0.7 copy-start.2
  173.4 0.7 copy-start.4
  226.7 0.6 copy-start.5
Sparse Core Ops, SparseCore 0:
  17.6 34.1 reduce-scatter.2
  180.6 29.6 reduce-scatter.4
Sparse Core Ops, SparseCore 1:
  20.2 127.7 all-gather.1
where the time goes:
time: 254 us; the launch traced here: 253 us
  waiting for transfers between devices  148 us (58%)
  blocking collectives  32 us (13%)
  local copies, waits for them, and re-layouts  21.3 us (8%)
  matrix products  19.2 us (8%)
  other arithmetic  16.6 us (7%)
  between operations  15.6 us (6%)
    all_gather x1, waiting for transfers between devices, local(): lax.all_gather(schur_inverse, 'col', axis=1, tiled=True)  85.5 us
    reduce_scatter x2, waiting for transfers between devices, local(): lax.psum_scatter(partial_rhs, 'row', scatter_dimension=1, tiled=True)  62.3 us
    all_gather x2, blocking collectives, local(): lax.all_gather(owned.astype(jnp.bfloat16), 'row', axis=1, tiled=True)  19.3 us
    all_gather x2, blocking collectives, local(): iface_full = lax.all_gather(iface_block, 'row', axis=1, tiled=True)  12.7 us
    dot_general x2, matrix products, local(): lax.dot_general(rhs_half, lax.all_gather(schur_inverse, 'col', axis=1, ti...  11.3 us
    scatter-add x2, other arithmetic, local(): partial_rhs = jax.ops.segment_sum(flat_values, flat_map, iface_width).T  7.77 us
    gather x2, local copies, waits for them, and re-layouts, local(): jnp.take(iface_full, flat_map, axis=1)  6.74 us
    all_gather x2, local copies, waits for them, and re-layouts, local(): iface_full = lax.all_gather(iface_block, 'row', axis=1, tiled=True)  5.81 us
  transfers between devices with their start and end apart: 3, of which 3 were waited for; matrix products, arithmetic and copies ran while one was open for 1% of the time, Pallas kernels for 0%

commit v1 on v0

v1 whole, which is shorter than its diff:
```python
import functools

import jax
import jax.numpy as jnp
from jax import lax
from jax.experimental import pallas as pl
from jax.experimental.pallas import tpu as pltpu
from jax.sharding import PartitionSpec as P

STEPS = 2
LANES = 128
MESH = pl.DeviceIdType.MESH
F32 = jnp.float32
BF16 = jnp.bfloat16


def halves(x):
    high = x.astype(BF16)
    low = (x - high.astype(F32)).astype(BF16)
    return jnp.concatenate([high, low], axis=0)


def joined(x, count):
    return x[:count].astype(F32) + x[count:].astype(F32)


def dot_nt(a, b):
    return lax.dot_general(a, b, (((1,), (1,)), ((), ())), preferred_element_type=F32)


def dot_nn(a, b):
    return lax.dot_general(a, b, (((1,), (0,)), ((), ())), preferred_element_type=F32)


def kernel(
    rows,
    cols,
    volt_ref,
    curr_ref,
    linv_hbm,
    schur_hbm,
    gain_ref,
    tie_ref,
    map_ref,
    breaker_ref,
    time_ref,
    node_ref,
    volt_out,
    curr_out,
    iface_out,
    linv,
    schur,
    open_volt,
    map_in,
    spread,
    pick,
    val_in,
    rhs_send,
    rhs_in,
    part_send,
    part_in,
    pick_send,
    pick_in,
    load_sem,
    send_sem,
    recv_sem,
):
    sub, scen, nodes = volt_ref.shape
    ports = tie_ref.shape[1]
    half = sub // 2
    own_i, own_j = schur.shape
    share = own_j // rows
    r = lax.axis_index("row")
    c = lax.axis_index("col")
    others = rows * cols - 1

    load_linv = pltpu.make_async_copy(linv_hbm, linv, load_sem.at[0])
    load_schur = pltpu.make_async_copy(schur_hbm, schur, load_sem.at[1])
    load_linv.start()
    load_schur.start()

    barrier = pltpu.get_barrier_semaphore()

    def greet(t, _):
        there = (lax.rem(r + t // cols, rows), lax.rem(c + lax.rem(t, cols), cols))
        pl.semaphore_signal(barrier, inc=1, device_id=there, device_id_type=MESH)
        return 0

    lax.fori_loop(1, rows * cols, greet, 0)

    def wait_bytes(ref, sem):
        pltpu.make_async_copy(ref, ref, sem).wait()

    def send(src, dst, phase, there):
        pltpu.make_async_remote_copy(
            src_ref=src,
            dst_ref=dst,
            send_sem=send_sem.at[phase],
            recv_sem=recv_sem.at[phase],
            device_id=there,
            device_id_type=MESH,
        ).start()

    def send_row(src_of, dst, phase):
        for d in range(1, rows):
            peer = lax.rem(r + d, rows)
            send(src_of(peer), dst, phase, (peer, c))

    scen_ids = lax.broadcasted_iota(jnp.int32, (scen, 1), 0)
    f_node = jnp.zeros((scen, 1), jnp.int32)
    f_time = jnp.zeros((scen, 1), jnp.int32)
    for s in range(scen):
        f_node = jnp.where(scen_ids == s, node_ref[s], f_node)
        f_time = jnp.where(scen_ids == s, time_ref[s], f_time)
    node_ids = lax.broadcasted_iota(jnp.int32, (scen, nodes), 1)

    def injection(step, k, volt, curr):
        closed = breaker_ref[k].astype(F32)
        hist = closed * (curr + gain_ref[k : k + 1, :] * volt)
        here = f_node - (r * sub + k) * nodes
        on = jnp.logical_and(node_ids == here, f_time <= step)
        fault_on = jnp.where(on, 1.0, 0.0).astype(F32)
        return (-hist - 2.0 * fault_on * volt).astype(BF16)

    def port_values(k):
        return tie_ref[k : k + 1, :] * open_volt[k, :, :ports]

    pl.semaphore_wait(barrier, others)
    send_row(lambda peer: map_ref, map_in.at[r], 0)
    map_in[r] = map_ref[...]
    load_linv.wait()

    for step in range(STEPS):
        base = 1 + 4 * step
        for k in range(sub):
            if step == 0:
                inject = injection(step, k, volt_ref[k], curr_ref[k])
            else:
                inject = injection(step, k, volt_out[k], curr_out[k])
            open_volt[k] = dot_nn(inject, linv[k])
        vals = jnp.concatenate(
            [
                jnp.concatenate([port_values(g), port_values(g + half)], axis=1)
                for g in range(half)
            ],
            axis=1,
        )
        val_in[step, r] = halves(vals)
        send_row(lambda peer: val_in.at[step, r], val_in.at[step, r], base)

        if step == 0:
            wait_bytes(map_in.at[pl.ds(0, rows - 1)], recv_sem.at[0])
            wait_bytes(map_in.at[pl.ds(0, rows - 1)], send_sem.at[0])
            ids = lax.broadcasted_iota(jnp.int32, (share, LANES), 0)

            def packed_map(q, g):
                m = map_in[q]
                return jnp.concatenate([m[g : g + 1], m[g + half : g + half + 1]], axis=1)

            def fill_spread(q, _):
                for g in range(half):
                    m = packed_map(q, g)
                    for b in range(cols):
                        hit = ids == m - (b * own_j + r * share)
                        spread[q, b * share : (b + 1) * share, g * LANES : (g + 1) * LANES] = (
                            jnp.where(hit, 1.0, 0.0).astype(BF16)
                        )
                return 0

            lax.fori_loop(0, rows, fill_spread, 0)

        wait_bytes(val_in.at[step, pl.ds(0, rows - 1)], recv_sem.at[base])
        rhs = dot_nt(val_in[step, 0], spread[0])
        for q in range(1, rows):
            rhs += dot_nt(val_in[step, q], spread[q])
        rhs = joined(rhs, scen).astype(BF16)
        for b in range(cols):
            rhs_send[step, b] = rhs[:, b * share : (b + 1) * share]

        def send_rhs(t, _):
            peer_r = lax.rem(r + t // cols, rows)
            peer_c = lax.rem(c + lax.rem(t, cols), cols)
            send(
                rhs_send.at[step, peer_c],
                rhs_in.at[step, r * cols + c],
                base + 1,
                (peer_r, peer_c),
            )
            return 0

        lax.fori_loop(1, rows * cols, send_rhs, 0)
        rhs_in[step, r * cols + c] = rhs_send[step, c]

        if step == 0:
            load_schur.wait()
            pick_ids = lax.broadcasted_iota(jnp.int32, (own_i, LANES), 0)

            def fill_pick(q, _):
                for g in range(half):
                    m = packed_map(q, g) - r * own_i
                    pick[q, :, g * LANES : (g + 1) * LANES] = jnp.where(
                        pick_ids == m, 1.0, 0.0
                    ).astype(BF16)
                return 0

            lax.fori_loop(0, rows, fill_pick, 0)

        wait_bytes(rhs_in.at[step, pl.ds(0, others)], recv_sem.at[base + 1])
        wide = jnp.concatenate(
            [
                rhs_in[step, q * cols : (q + 1) * cols].reshape(cols * scen, share)
                for q in range(rows)
            ],
            axis=1,
        )
        part = dot_nt(wide, schur[...]).astype(BF16)
        part_send[step] = part.reshape(cols, scen, own_i)
        for d in range(1, cols):
            peer = lax.rem(c + d, cols)
            send(part_send.at[step, peer], part_in.at[step, c], base + 2, (r, peer))
        part_in[step, c] = part_send[step, c]

        wait_bytes(part_in.at[step, pl.ds(0, cols - 1)], recv_sem.at[base + 2])
        iface = part_in[step, 0].astype(F32)
        for b in range(1, cols):
            iface += part_in[step, b].astype(F32)
        if step == STEPS - 1:
            iface_out[...] = iface
        iface_halves = halves(iface)
        for q in range(rows):
            pick_send[step, q] = dot_nn(iface_halves, pick[q]).astype(BF16)
        send_row(lambda peer: pick_send.at[step, peer], pick_in.at[step, r], base + 3)
        pick_in[step, r] = pick_send[step, r]
        wait_bytes(pick_in.at[step, pl.ds(0, rows - 1)], recv_sem.at[base + 3])
        picked = joined(pick_in[step, 0], scen)
        for q in range(1, rows):
            picked += joined(pick_in[step, q], scen)

        for k in range(sub):
            first = (k % half) * LANES + (k // half) * ports
            drive = (tie_ref[k : k + 1, :] * picked[:, first : first + ports]).astype(BF16)
            volt_next = open_volt[k] + dot_nn(drive, linv[k, :ports, :])
            if step == 0:
                volt, curr = volt_ref[k], curr_ref[k]
            else:
                volt, curr = volt_out[k], curr_out[k]
            closed = breaker_ref[k].astype(F32)
            curr_out[k] = closed * (curr + gain_ref[k : k + 1, :] * (volt_next + volt))
            volt_out[k] = volt_next

        wait_bytes(val_in.at[step, pl.ds(0, rows - 1)], send_sem.at[base])
        wait_bytes(rhs_in.at[step, pl.ds(0, others)], send_sem.at[base + 1])
        wait_bytes(part_in.at[step, pl.ds(0, cols - 1)], send_sem.at[base + 2])
        wait_bytes(pick_in.at[step, pl.ds(0, rows - 1)], send_sem.at[base + 3])


def fused(
    volt_init,
    curr_init,
    local_inverse,
    schur_inverse,
    ind_gain,
    tie,
    port_map,
    breaker,
    fault_time,
    fault_node,
):
    rows, cols = lax.axis_size("row"), lax.axis_size("col")
    sub, scen, nodes = volt_init.shape
    ports = tie.shape[1]
    own_i, own_j = schur_inverse.shape
    share = own_j // rows
    flat = sub * ports
    vmem = pl.BlockSpec(memory_space=pltpu.VMEM)
    smem = pl.BlockSpec(memory_space=pltpu.SMEM)
    anywhere = pl.BlockSpec(memory_space=pl.ANY)
    return pl.pallas_call(
        functools.partial(kernel, rows, cols),
        out_shape=(
            jax.ShapeDtypeStruct(volt_init.shape, F32),
            jax.ShapeDtypeStruct(volt_init.shape, F32),
            jax.ShapeDtypeStruct((scen, own_i), F32),
        ),
        in_specs=[vmem, vmem, anywhere, anywhere, vmem, vmem, vmem, vmem, smem, smem],
        out_specs=(vmem, vmem, vmem),
        scratch_shapes=[
            pltpu.VMEM(local_inverse.shape, BF16),
            pltpu.VMEM(schur_inverse.shape, BF16),
            pltpu.VMEM(volt_init.shape, F32),
            pltpu.VMEM((rows, sub, ports), jnp.int32),
            pltpu.VMEM((rows, cols * share, flat), BF16),
            pltpu.VMEM((rows, own_i, flat), BF16),
            pltpu.VMEM((STEPS, rows, 2 * scen, flat), BF16),
            pltpu.VMEM((STEPS, cols, scen, share), BF16),
            pltpu.VMEM((STEPS, rows * cols, scen, share), BF16),
            pltpu.VMEM((STEPS, cols, scen, own_i), BF16),
            pltpu.VMEM((STEPS, cols, scen, own_i), BF16),
            pltpu.VMEM((STEPS, rows, 2 * scen, flat), BF16),
            pltpu.VMEM((STEPS, rows, 2 * scen, flat), BF16),
            pltpu.SemaphoreType.DMA((2,)),
            pltpu.SemaphoreType.DMA((1 + 4 * STEPS,)),
            pltpu.SemaphoreType.DMA((1 + 4 * STEPS,)),
        ],
        compiler_params=pltpu.CompilerParams(
            collective_id=0, has_side_effects=True, vmem_limit_bytes=48 * 1024 * 1024
        ),
    )(
        volt_init,
        curr_init,
        local_inverse,
        schur_inverse,
        ind_gain,
        tie,
        port_map,
        breaker,
        fault_time,
        fault_node,
    )


def plain(
    volt_init,
    curr_init,
    local_inverse,
    schur_inverse,
    ind_gain,
    tie,
    port_map,
    breaker,
    fault_time,
    fault_node,
):
    sub_count, scen_count, node_count = volt_init.shape
    port_count = tie.shape[1]
    iface_width = lax.axis_size("row") * schur_inverse.shape[0]
    volt = volt_init
    curr = curr_init
    closed = breaker.astype(F32)
    first_sub = lax.axis_index("row") * sub_count
    node_ids = (first_sub + jnp.arange(sub_count, dtype=jnp.int32))[
        :, None
    ] * node_count + jnp.arange(node_count, dtype=jnp.int32)[None, :]
    hits = node_ids[:, None, :] == fault_node[None, :, None]
    flat_map = port_map.reshape(-1)
    port_inverse = local_inverse[:, :port_count, :]
    iface_block = jnp.zeros((scen_count, schur_inverse.shape[0]), F32)
    for step in range(STEPS):
        hist = closed * (curr + ind_gain[:, None, :] * volt)
        active = (step >= fault_time)[None, :, None]
        fault_on = jnp.where(hits & active, 1.0, 0.0).astype(F32)
        inject = (-hist - 2.0 * fault_on * volt).astype(BF16)
        open_volt = jnp.einsum("ksn,knm->ksm", inject, local_inverse, preferred_element_type=F32)
        values = tie[:, None, :] * open_volt[:, :, :port_count]
        flat_values = jnp.transpose(values, (0, 2, 1)).reshape(sub_count * port_count, scen_count)
        partial_rhs = jax.ops.segment_sum(flat_values, flat_map, iface_width).T
        owned = lax.psum_scatter(partial_rhs, "row", scatter_dimension=1, tiled=True)
        rhs_half = lax.all_gather(owned.astype(BF16), "row", axis=1, tiled=True)
        iface_block = dot_nt(rhs_half, lax.all_gather(schur_inverse, "col", axis=1, tiled=True))
        iface_full = lax.all_gather(iface_block, "row", axis=1, tiled=True)
        picked = jnp.take(iface_full, flat_map, axis=1).reshape(scen_count, sub_count, port_count)
        drive = (tie[:, None, :] * jnp.transpose(picked, (1, 0, 2))).astype(BF16)
        volt_next = open_volt + jnp.einsum(
            "ksp,kpn->ksn", drive, port_inverse, preferred_element_type=F32
        )
        curr = closed * (curr + ind_gain[:, None, :] * (volt_next + volt))
        volt = volt_next
    return (volt, curr, iface_block)


def local(*args):
    volt_init, schur_inverse, tie = args[0], args[3], args[5]
    sub, scen, _ = volt_init.shape
    own_i, own_j = schur_inverse.shape
    aligned = (
        own_j % (lax.axis_size("row") * LANES) == 0
        and own_i % LANES == 0
        and scen % 16 == 0
        and sub % 2 == 0
        and 2 * tie.shape[1] == LANES
    )
    return fused(*args) if aligned else plain(*args)


def solution(mesh):
    placed = (
        P("row", "col", None),
        P("row", "col", None),
        P("row", None, None),
        P("row", "col"),
        P("row", None),
        P("row", None),
        P("row", None),
        P("row", "col", None),
        P("col"),
        P("col"),
    )
    return jax.shard_map(
        local,
        mesh=mesh,
        in_specs=placed,
        out_specs=(P("row", "col", None), P("row", "col", None), P("col", "row")),
        check_vma=False,
    )
```

time: 254 us -> 64.5 us (0.25)
  waiting for transfers between devices: 148 us -> 0 us
  Pallas kernels: 0 us -> 52 us
  blocking collectives: 32 us -> 0 us
  matrix products: 19.2 us -> 0 us
  other arithmetic: 16.6 us -> 0 us
  between operations: 15.6 us -> 0.66 us
  local copies, waits for them, and re-layouts: 21.3 us -> 11.4 us
    all_gather x1 -> x0, waiting for transfers between devices: 85.5 us -> none  [local(): lax.all_gather(schur_inverse, 'col', axis=1, tiled=True)]
    reduce_scatter x2 -> x0, waiting for transfers between devices: 62.3 us -> none  [local(): lax.psum_scatter(partial_rhs, 'row', scatter_dimension=1, tiled=True)]
    pallas_call x0 -> x1, Pallas kernels: none -> 52 us  [fused(): pl.pallas_call(functools.partial(kernel, rows, cols), out_shape=(jax.Shap...]
    all_gather x4 -> x0, blocking collectives: 32 us -> none  [the longest x2 19.3 us: local(): lax.all_gather(owned.astype(jnp.bfloat16), 'row', axis=1, tiled=True)]
    dot_general x6 -> x0, matrix products: 19.2 us -> none  [the longest x2 11.3 us: local(): lax.dot_general(rhs_half, lax.all_gather(schur_inverse, 'col', axis=1, ti...]
    unnamed x22 -> x23, local copies, waits for them, and re-layouts: 2.8 us -> 11.4 us
    scatter-add x2 -> x0, other arithmetic: 7.77 us -> none  [local(): partial_rhs = jax.ops.segment_sum(flat_values, flat_map, iface_width).T]
    gather x2 -> x0, local copies, waits for them, and re-layouts: 6.74 us -> none  [local(): jnp.take(iface_full, flat_map, axis=1)]
  transfers between devices with their start and end apart: 3 -> 0, of which waited for: 3 -> 0; matrix products, arithmetic and copies ran while one was open for 1% -> 0% of each run, Pallas kernels for 0% -> 0%
where the time goes in v1:
time: 64.5 us; the launch traced here: 64.1 us
  Pallas kernels  52 us (81%)
  local copies, waits for them, and re-layouts  11.4 us (18%)
  between operations  0.66 us (1%)
    pallas_call x1, Pallas kernels, fused(): pl.pallas_call(functools.partial(kernel, rows, cols), out_shape=(jax.Shap...  52 us
    unnamed x23, local copies, waits for them, and re-layouts  11.4 us

profile of v1, /device:TPU:0, one launch (start us, length us, event | category | flops | bytes accessed | tf_op | source)
XLA Modules:
  0.0 64.1 jit_solution(1160452311433249681)
XLA Ops:
  0.6 0.0 copy-start
  0.6 1.9 %copy-done = bf16[8,400,400]{2,1,0:T(8,128)(2,1)S(1)} copy-done((bf16[8,400,400]{2,1,0:T(8,128)(2,1)S(1)}, bf16[8,400,400]{2,1,0:T(8,128)(2,1)}, u32[]{:S(2)}) %copy-start) | copy-done | bytes 2560024
  2.6 0.0 copy-start.1
  2.6 1.2 %copy-done.1 = bf16[1024,512]{1,0:T(8,128)(2,1)S(1)} copy-done((bf16[1024,512]{1,0:T(8,128)(2,1)S(1)}, bf16[1024,512]{1,0:T(8,128)(2,1)}, u32[]{:S(2)}) %copy-start.1) | copy-done | bytes 1048600
  3.8 0.0 copy-start.2
  3.8 0.9 %copy-done.2 = f32[8,16,400]{2,1,0:T(8,128)S(1)} copy-done((f32[8,16,400]{2,1,0:T(8,128)S(1)}, f32[8,16,400]{2,1,0:T(8,128)}, u32[]{:S(2)}) %copy-start.2) | copy-done | bytes 204824
  4.7 0.0 copy-start.3
  4.7 0.9 %copy-done.3 = f32[8,16,400]{2,1,0:T(8,128)S(1)} copy-done((f32[8,16,400]{2,1,0:T(8,128)S(1)}, f32[8,16,400]{2,1,0:T(8,128)}, u32[]{:S(2)}) %copy-start.3) | copy-done | bytes 204824
  5.7 0.0 copy-start.4
  5.7 0.9 %copy-done.4 = s32[8,16,400]{2,1,0:T(8,128)S(1)} copy-done((s32[8,16,400]{2,1,0:T(8,128)S(1)}, s32[8,16,400]{2,1,0:T(8,128)}, u32[]{:S(2)}) %copy-start.4) | copy-done | bytes 204824
  6.6 0.0 copy-start.5
  6.6 0.7 %copy-done.5 = f32[8,400]{1,0:T(8,128)S(1)} copy-done((f32[8,400]{1,0:T(8,128)S(1)}, f32[8,400]{1,0:T(8,128)}, u32[]{:S(2)}) %copy-start.5) | copy-done | bytes 12824
  7.4 0.0 copy-start.6
  7.4 0.7 %copy-done.6 = f32[8,64]{1,0:T(8,128)S(1)} copy-done((f32[8,64]{1,0:T(8,128)S(1)}, f32[8,64]{1,0:T(8,128)}, u32[]{:S(2)}) %copy-start.6) | copy-done | bytes 2072
  8.0 0.0 copy-start.7
  8.0 0.7 %copy-done.7 = s32[8,64]{1,0:T(8,128)S(1)} copy-done((s32[8,64]{1,0:T(8,128)S(1)}, s32[8,64]{1,0:T(8,128)}, u32[]{:S(2)}) %copy-start.7) | copy-done | bytes 2072
  8.7 0.0 copy-start.8
  8.7 0.7 %copy-done.8 = s32[16]{0:T(128)S(1)} copy-done((s32[16]{0:T(128)S(1)}, s32[16]{0:T(128)}, u32[]{:S(2)}) %copy-start.8) | copy-done | bytes 88
  9.4 0.0 copy-start.9
  9.4 0.7 %copy-done.9 = s32[16]{0:T(128)S(1)} copy-done((s32[16]{0:T(128)S(1)}, s32[16]{0:T(128)}, u32[]{:S(2)}) %copy-start.9) | copy-done | bytes 88
  10.0 52.0 %shard_map.121 = (f32[8,16,400]{2,1,0:T(8,128)S(1)}, f32[8,16,400]{2,1,0:T(8,128)S(1)}, f32[16,1024]{1,0:T(8,128)S(1)}) custom-call(f32[8,16,400]{2,1,0:T(8,128)S(1)} %copy-done.2, f32[8,16,400]{2,1,0:T(8,128)S(1)} %copy-done.3, bf16[8,400,400]{2,1,0:T(8,128)(2,1)S(1)} %copy-done, bf16[1024,512]{1,0:T(8,128)(2,1)S(1)} %copy-done.1, f32[8,400]{1,0:T(8,128)S(1)} %copy-done.5, ...), custom_call_target="tpu_custom_call" | custom-call | tf_op jit(solution)/shard_map/pallas_call | solution.py:278
  62.1 0.7 %copy.16 = f32[8,16,400]{2,1,0:T(8,128)} copy(f32[8,16,400]{2,1,0:T(8,128)S(1)} %get-tuple-element.6) | data formatting | bytes 409600
  62.8 0.7 %copy.17 = f32[8,16,400]{2,1,0:T(8,128)} copy(f32[8,16,400]{2,1,0:T(8,128)S(1)} %get-tuple-element.7) | data formatting | bytes 409600
  63.5 0.6 copy.18
Async XLA Ops:
  0.6 1.9 %copy-start = (bf16[8,400,400]{2,1,0:T(8,128)(2,1)S(1)}, bf16[8,400,400]{2,1,0:T(8,128)(2,1)}, u32[]{:S(2)}) copy-start(bf16[8,400,400]{2,1,0:T(8,128)(2,1)} %linv_hbm.1) | copy-start | bytes 7680004
  2.6 1.2 %copy-start.1 = (bf16[1024,512]{1,0:T(8,128)(2,1)S(1)}, bf16[1024,512]{1,0:T(8,128)(2,1)}, u32[]{:S(2)}) copy-start(bf16[1024,512]{1,0:T(8,128)(2,1)} %schur_hbm.1) | copy-start | bytes 3145732
  3.8 0.9 %copy-start.2 = (f32[8,16,400]{2,1,0:T(8,128)S(1)}, f32[8,16,400]{2,1,0:T(8,128)}, u32[]{:S(2)}) copy-start(f32[8,16,400]{2,1,0:T(8,128)} %volt_ref.1) | copy-start | bytes 614404
  4.7 0.9 %copy-start.3 = (f32[8,16,400]{2,1,0:T(8,128)S(1)}, f32[8,16,400]{2,1,0:T(8,128)}, u32[]{:S(2)}) copy-start(f32[8,16,400]{2,1,0:T(8,128)} %curr_ref.1) | copy-start | bytes 614404
  5.7 0.9 %copy-start.4 = (s32[8,16,400]{2,1,0:T(8,128)S(1)}, s32[8,16,400]{2,1,0:T(8,128)}, u32[]{:S(2)}) copy-start(s32[8,16,400]{2,1,0:T(8,128)} %breaker_ref.1) | copy-start | bytes 614404
  6.6 0.7 %copy-start.5 = (f32[8,400]{1,0:T(8,128)S(1)}, f32[8,400]{1,0:T(8,128)}, u32[]{:S(2)}) copy-start(f32[8,400]{1,0:T(8,128)} %gain_ref.1) | copy-start | bytes 38404
  7.4 0.7 %copy-start.6 = (f32[8,64]{1,0:T(8,128)S(1)}, f32[8,64]{1,0:T(8,128)}, u32[]{:S(2)}) copy-start(f32[8,64]{1,0:T(8,128)} %tie_ref.1) | copy-start | bytes 6148
  8.0 0.7 %copy-start.7 = (s32[8,64]{1,0:T(8,128)S(1)}, s32[8,64]{1,0:T(8,128)}, u32[]{:S(2)}) copy-start(s32[8,64]{1,0:T(8,128)} %map_ref.1) | copy-start | bytes 6148
  8.7 0.7 %copy-start.8 = (s32[16]{0:T(128)S(1)}, s32[16]{0:T(128)}, u32[]{:S(2)}) copy-start(s32[16]{0:T(128)} %time_ref.1) | copy-start | bytes 196
  9.4 0.7 %copy-start.9 = (s32[16]{0:T(128)S(1)}, s32[16]{0:T(128)}, u32[]{:S(2)}) copy-start(s32[16]{0:T(128)} %node_ref.1) | copy-start | bytes 196

commit v2 on v1

--- a/solution.py
+++ b/solution.py
@@ -8,6 +8,7 @@
 from jax.sharding import PartitionSpec as P
 
 STEPS = 2
+PIECES = 2
 LANES = 128
 MESH = pl.DeviceIdType.MESH
 F32 = jnp.float32
@@ -35,21 +36,29 @@
 def kernel(
     rows,
     cols,
+    volt_hbm,
+    curr_hbm,
+    linv_hbm,
+    schur_hbm,
+    gain_hbm,
+    tie_hbm,
+    map_hbm,
+    breaker_hbm,
+    time_hbm,
+    node_hbm,
+    volt_out,
+    curr_out,
+    iface_out,
     volt_ref,
     curr_ref,
-    linv_hbm,
-    schur_hbm,
+    linv,
+    schur,
     gain_ref,
     tie_ref,
     map_ref,
     breaker_ref,
     time_ref,
     node_ref,
-    volt_out,
-    curr_out,
-    iface_out,
-    linv,
-    schur,
     open_volt,
     map_in,
     spread,
@@ -64,20 +73,37 @@
     load_sem,
     send_sem,
     recv_sem,
+    val_sem,
 ):
     sub, scen, nodes = volt_ref.shape
     ports = tie_ref.shape[1]
     half = sub // 2
     own_i, own_j = schur.shape
     share = own_j // rows
+    piece = own_i // PIECES
     r = lax.axis_index("row")
     c = lax.axis_index("col")
     others = rows * cols - 1
 
-    load_linv = pltpu.make_async_copy(linv_hbm, linv, load_sem.at[0])
-    load_schur = pltpu.make_async_copy(schur_hbm, schur, load_sem.at[1])
-    load_linv.start()
-    load_schur.start()
+    loads = [
+        pltpu.make_async_copy(src, dst, load_sem.at[n])
+        for n, (src, dst) in enumerate(
+            (
+                (time_hbm, time_ref),
+                (node_hbm, node_ref),
+                (gain_hbm, gain_ref),
+                (tie_hbm, tie_ref),
+                (map_hbm, map_ref),
+                (volt_hbm, volt_ref),
+                (curr_hbm, curr_ref),
+                (breaker_hbm, breaker_ref),
+                (linv_hbm, linv),
+                (schur_hbm, schur),
+            )
+        )
+    ]
+    for load in loads:
+        load.start()
 
     barrier = pltpu.get_barrier_semaphore()
 
@@ -87,24 +113,26 @@
         return 0
 
     lax.fori_loop(1, rows * cols, greet, 0)
+    for load in loads[:-1]:
+        load.wait()
 
     def wait_bytes(ref, sem):
         pltpu.make_async_copy(ref, ref, sem).wait()
 
-    def send(src, dst, phase, there):
+    def send(src, dst, phase, there, recv=None):
         pltpu.make_async_remote_copy(
             src_ref=src,
             dst_ref=dst,
             send_sem=send_sem.at[phase],
-            recv_sem=recv_sem.at[phase],
+            recv_sem=recv_sem.at[phase] if recv is None else recv,
             device_id=there,
             device_id_type=MESH,
         ).start()
 
-    def send_row(src_of, dst, phase):
-        for d in range(1, rows):
-            peer = lax.rem(r + d, rows)
-            send(src_of(peer), dst, phase, (peer, c))
+    def row_peer(d):
+        return lax.rem(r + d, rows)
+
+    far_first = sorted(range(1, rows), key=lambda d: abs(d - rows // 2))
 
     scen_ids = lax.broadcasted_iota(jnp.int32, (scen, 1), 0)
     f_node = jnp.zeros((scen, 1), jnp.int32)
@@ -122,22 +150,45 @@
         fault_on = jnp.where(on, 1.0, 0.0).astype(F32)
         return (-hist - 2.0 * fault_on * volt).astype(BF16)
 
-    def port_values(k):
-        return tie_ref[k : k + 1, :] * open_volt[k, :, :ports]
-
-    pl.semaphore_wait(barrier, others)
-    send_row(lambda peer: map_ref, map_in.at[r], 0)
-    map_in[r] = map_ref[...]
-    load_linv.wait()
+    ids = lax.broadcasted_iota(jnp.int32, (LANES, LANES), 0).astype(F32).astype(BF16)
+    one = jnp.ones((LANES, LANES), BF16)
+    zero = jnp.zeros((LANES, LANES), BF16)
+
+    def hits(m):
+        near = jnp.clip(m, -1, LANES).astype(F32).astype(BF16)
+        return jnp.where(ids == near, one, zero)
+
+    def packed_map(m, g):
+        return jnp.concatenate([m[g : g + 1], m[g + half : g + half + 1]], axis=1)
+
+    def fill_spread(q, maps):
+        for g in range(half):
+            m = packed_map(maps, g)
+            for b in range(cols):
+                for e in range(share // LANES):
+                    first = b * share + e * LANES
+                    spread[q, first : first + LANES, g * LANES : (g + 1) * LANES] = hits(
+                        m - (b * own_j + r * share + e * LANES)
+                    )
+
+    def fill_pick(q, maps):
+        for g in range(half):
+            m = packed_map(maps, g) - r * own_i
+            for e in range(own_i // LANES):
+                pick[q, e * LANES : (e + 1) * LANES, g * LANES : (g + 1) * LANES] = hits(
+                    m - e * LANES
+                )
 
     for step in range(STEPS):
-        base = 1 + 4 * step
+        base = 1 + (3 + PIECES) * step
+        volt_now, curr_now = (volt_ref, curr_ref) if step == 0 else (volt_out, curr_out)
+        injects = [injection(step, k, volt_now[k], curr_now[k]) for k in range(sub)]
         for k in range(sub):
-            if step == 0:
-                inject = injection(step, k, volt_ref[k], curr_ref[k])
-            else:
-                inject = injection(step, k, volt_out[k], curr_out[k])
-            open_volt[k] = dot_nn(inject, linv[k])
+            open_volt[k] = dot_nn(injects[k], linv[k])
+
+        def port_values(k):
+            return tie_ref[k : k + 1, :] * open_volt[k, :, :ports]
+
         vals = jnp.concatenate(
             [
                 jnp.concatenate([port_values(g), port_values(g + half)], axis=1)
@@ -146,32 +197,29 @@
             axis=1,
         )
         val_in[step, r] = halves(vals)
-        send_row(lambda peer: val_in.at[step, r], val_in.at[step, r], base)
-
         if step == 0:
+            pl.semaphore_wait(barrier, others)
+            for d in far_first:
+                send(map_ref, map_in.at[r], 0, (row_peer(d), c))
+        for d in far_first:
+            mine = val_in.at[step, r]
+            send(mine, mine, base, (row_peer(d), c), val_sem.at[step, d - 1])
+
+        if step == 0:
+            fill_spread(r, map_ref[...])
+            fill_pick(r, map_ref[...])
             wait_bytes(map_in.at[pl.ds(0, rows - 1)], recv_sem.at[0])
-            wait_bytes(map_in.at[pl.ds(0, rows - 1)], send_sem.at[0])
-            ids = lax.broadcasted_iota(jnp.int32, (share, LANES), 0)
-
-            def packed_map(q, g):
-                m = map_in[q]
-                return jnp.concatenate([m[g : g + 1], m[g + half : g + half + 1]], axis=1)
-
-            def fill_spread(q, _):
-                for g in range(half):
-                    m = packed_map(q, g)
-                    for b in range(cols):
-                        hit = ids == m - (b * own_j + r * share)
-                        spread[q, b * share : (b + 1) * share, g * LANES : (g + 1) * LANES] = (
-                            jnp.where(hit, 1.0, 0.0).astype(BF16)
-                        )
+
+            def fill_rest(d, _):
+                fill_spread(row_peer(d), map_in[row_peer(d)])
                 return 0
 
-            lax.fori_loop(0, rows, fill_spread, 0)
-
-        wait_bytes(val_in.at[step, pl.ds(0, rows - 1)], recv_sem.at[base])
-        rhs = dot_nt(val_in[step, 0], spread[0])
-        for q in range(1, rows):
+            lax.fori_loop(1, rows, fill_rest, 0)
+
+        rhs = dot_nt(val_in[step, r], spread[r])
+        for d in reversed(far_first):
+            q = row_peer(rows - d)
+            wait_bytes(val_in.at[step, q], val_sem.at[step, d - 1])
             rhs += dot_nt(val_in[step, q], spread[q])
         rhs = joined(rhs, scen).astype(BF16)
         for b in range(cols):
@@ -192,18 +240,13 @@
         rhs_in[step, r * cols + c] = rhs_send[step, c]
 
         if step == 0:
-            load_schur.wait()
-            pick_ids = lax.broadcasted_iota(jnp.int32, (own_i, LANES), 0)
-
-            def fill_pick(q, _):
-                for g in range(half):
-                    m = packed_map(q, g) - r * own_i
-                    pick[q, :, g * LANES : (g + 1) * LANES] = jnp.where(
-                        pick_ids == m, 1.0, 0.0
-                    ).astype(BF16)
+
+            def fill_rest_pick(d, _):
+                fill_pick(row_peer(d), map_in[row_peer(d)])
                 return 0
 
-            lax.fori_loop(0, rows, fill_pick, 0)
+            lax.fori_loop(1, rows, fill_rest_pick, 0)
+            loads[-1].wait()
 
         wait_bytes(rhs_in.at[step, pl.ds(0, others)], recv_sem.at[base + 1])
         wide = jnp.concatenate(
@@ -213,45 +256,71 @@
             ],
             axis=1,
         )
-        part = dot_nt(wide, schur[...]).astype(BF16)
-        part_send[step] = part.reshape(cols, scen, own_i)
-        for d in range(1, cols):
-            peer = lax.rem(c + d, cols)
-            send(part_send.at[step, peer], part_in.at[step, c], base + 2, (r, peer))
-        part_in[step, c] = part_send[step, c]
-
-        wait_bytes(part_in.at[step, pl.ds(0, cols - 1)], recv_sem.at[base + 2])
-        iface = part_in[step, 0].astype(F32)
-        for b in range(1, cols):
-            iface += part_in[step, b].astype(F32)
-        if step == STEPS - 1:
-            iface_out[...] = iface
-        iface_halves = halves(iface)
-        for q in range(rows):
-            pick_send[step, q] = dot_nn(iface_halves, pick[q]).astype(BF16)
-        send_row(lambda peer: pick_send.at[step, peer], pick_in.at[step, r], base + 3)
-        pick_in[step, r] = pick_send[step, r]
-        wait_bytes(pick_in.at[step, pl.ds(0, rows - 1)], recv_sem.at[base + 3])
+        for h in range(PIECES):
+            part = dot_nt(wide, schur[h * piece : (h + 1) * piece, :]).astype(BF16)
+            part_send[step, h] = part.reshape(cols, scen, piece)
+            for d in range(1, cols):
+                peer = lax.rem(c + d, cols)
+                send(
+                    part_send.at[step, h, peer],
+                    part_in.at[step, h, c],
+                    base + 2 + h,
+                    (r, peer),
+                )
+            part_in[step, h, c] = part_send[step, h, c]
+
+        def summed(h):
+            wait_bytes(part_in.at[step, h, pl.ds(0, cols - 1)], recv_sem.at[base + 2 + h])
+            iface = part_in[step, h, 0].astype(F32)
+            for b in range(1, cols):
+                iface += part_in[step, h, b].astype(F32)
+            if step == STEPS - 1:
+                iface_out[:, h * piece : (h + 1) * piece] = iface
+            return halves(iface)
+
+        order = far_first + [0]
+        totals = {}
+        for h in range(PIECES):
+            iface = summed(h)
+            for d in order:
+                q = row_peer(d)
+                term = dot_nn(iface, pick[q, h * piece : (h + 1) * piece, :])
+                totals[d] = term if h == 0 else totals[d] + term
+                if h == PIECES - 1:
+                    if d == 0:
+                        pick_in[step, r] = totals[d].astype(BF16)
+                    else:
+                        pick_send[step, q] = totals[d].astype(BF16)
+                        send(
+                            pick_send.at[step, q],
+                            pick_in.at[step, r],
+                            base + 2 + PIECES,
+                            (q, c),
+                        )
+        wait_bytes(pick_in.at[step, pl.ds(0, rows - 1)], recv_sem.at[base + 2 + PIECES])
         picked = joined(pick_in[step, 0], scen)
         for q in range(1, rows):
             picked += joined(pick_in[step, q], scen)
 
+        drives = []
         for k in range(sub):
             first = (k % half) * LANES + (k // half) * ports
-            drive = (tie_ref[k : k + 1, :] * picked[:, first : first + ports]).astype(BF16)
-            volt_next = open_volt[k] + dot_nn(drive, linv[k, :ports, :])
-            if step == 0:
-                volt, curr = volt_ref[k], curr_ref[k]
-            else:
-                volt, curr = volt_out[k], curr_out[k]
+            drives.append((tie_ref[k : k + 1, :] * picked[:, first : first + ports]).astype(BF16))
+        for k in range(sub):
+            volt, curr = volt_now[k], curr_now[k]
+            volt_next = open_volt[k] + dot_nn(drives[k], linv[k, :ports, :])
             closed = breaker_ref[k].astype(F32)
             curr_out[k] = closed * (curr + gain_ref[k : k + 1, :] * (volt_next + volt))
             volt_out[k] = volt_next
 
+    wait_bytes(map_in.at[pl.ds(0, rows - 1)], send_sem.at[0])
+    for step in range(STEPS):
+        base = 1 + (3 + PIECES) * step
         wait_bytes(val_in.at[step, pl.ds(0, rows - 1)], send_sem.at[base])
         wait_bytes(rhs_in.at[step, pl.ds(0, others)], send_sem.at[base + 1])
-        wait_bytes(part_in.at[step, pl.ds(0, cols - 1)], send_sem.at[base + 2])
-        wait_bytes(pick_in.at[step, pl.ds(0, rows - 1)], send_sem.at[base + 3])
+        for h in range(PIECES):
+            wait_bytes(part_in.at[step, h, pl.ds(0, cols - 1)], send_sem.at[base + 2 + h])
+        wait_bytes(pick_in.at[step, pl.ds(0, rows - 1)], send_sem.at[base + 2 + PIECES])
 
 
 def fused(
@@ -273,8 +342,7 @@
     share = own_j // rows
     flat = sub * ports
     vmem = pl.BlockSpec(memory_space=pltpu.VMEM)
-    smem = pl.BlockSpec(memory_space=pltpu.SMEM)
-    anywhere = pl.BlockSpec(memory_space=pl.ANY)
+    hbm = pl.BlockSpec(memory_space=pltpu.HBM)
     return pl.pallas_call(
         functools.partial(kernel, rows, cols),
         out_shape=(
@@ -282,11 +350,19 @@
             jax.ShapeDtypeStruct(volt_init.shape, F32),
             jax.ShapeDtypeStruct((scen, own_i), F32),
         ),
-        in_specs=[vmem, vmem, anywhere, anywhere, vmem, vmem, vmem, vmem, smem, smem],
+        in_specs=[hbm] * 10,
         out_specs=(vmem, vmem, vmem),
         scratch_shapes=[
+            pltpu.VMEM(volt_init.shape, F32),
+            pltpu.VMEM(volt_init.shape, F32),
             pltpu.VMEM(local_inverse.shape, BF16),
             pltpu.VMEM(schur_inverse.shape, BF16),
+            pltpu.VMEM(ind_gain.shape, F32),
+            pltpu.VMEM(tie.shape, F32),
+            pltpu.VMEM(port_map.shape, jnp.int32),
+            pltpu.VMEM(breaker.shape, jnp.int32),
+            pltpu.SMEM(fault_time.shape, jnp.int32),
+            pltpu.SMEM(fault_node.shape, jnp.int32),
             pltpu.VMEM(volt_init.shape, F32),
             pltpu.VMEM((rows, sub, ports), jnp.int32),
             pltpu.VMEM((rows, cols * share, flat), BF16),
@@ -294,16 +370,17 @@
             pltpu.VMEM((STEPS, rows, 2 * scen, flat), BF16),
             pltpu.VMEM((STEPS, cols, scen, share), BF16),
             pltpu.VMEM((STEPS, rows * cols, scen, share), BF16),
-            pltpu.VMEM((STEPS, cols, scen, own_i), BF16),
-            pltpu.VMEM((STEPS, cols, scen, own_i), BF16),
+            pltpu.VMEM((STEPS, PIECES, cols, scen, own_i // PIECES), BF16),
+            pltpu.VMEM((STEPS, PIECES, cols, scen, own_i // PIECES), BF16),
             pltpu.VMEM((STEPS, rows, 2 * scen, flat), BF16),
             pltpu.VMEM((STEPS, rows, 2 * scen, flat), BF16),
-            pltpu.SemaphoreType.DMA((2,)),
-            pltpu.SemaphoreType.DMA((1 + 4 * STEPS,)),
-            pltpu.SemaphoreType.DMA((1 + 4 * STEPS,)),
+            pltpu.SemaphoreType.DMA((10,)),
+            pltpu.SemaphoreType.DMA((1 + (3 + PIECES) * STEPS,)),
+            pltpu.SemaphoreType.DMA((1 + (3 + PIECES) * STEPS,)),
+            pltpu.SemaphoreType.DMA((STEPS, rows - 1)),
         ],
         compiler_params=pltpu.CompilerParams(
-            collective_id=0, has_side_effects=True, vmem_limit_bytes=48 * 1024 * 1024
+            collective_id=0, has_side_effects=True, vmem_limit_bytes=60 * 1024 * 1024
         ),
     )(
         volt_init,
@@ -374,7 +451,7 @@
     own_i, own_j = schur_inverse.shape
     aligned = (
         own_j % (lax.axis_size("row") * LANES) == 0
-        and own_i % LANES == 0
+        and own_i % (PIECES * LANES) == 0
         and scen % 16 == 0
         and sub % 2 == 0
         and 2 * tie.shape[1] == LANES

time: 64.5 us -> 57.3 us (0.89)
  local copies, waits for them, and re-layouts: 11.4 us -> 4.81 us
    unnamed x23 -> x3, local copies, waits for them, and re-layouts: 11.4 us -> 4.81 us
where the time goes in v2:
time: 57.3 us; the launch traced here: 57.1 us
  Pallas kernels  51.6 us (90%)
  local copies, waits for them, and re-layouts  4.81 us (8%)
  between operations  0.64 us (1%)
    pallas_call x1, Pallas kernels, fused(): pl.pallas_call(functools.partial(kernel, rows, cols), out_shape=(jax.Shap...  51.6 us
    unnamed x3, local copies, waits for them, and re-layouts  4.81 us

profile of v2, /device:TPU:0, one launch (start us, length us, event | category | flops | bytes accessed | tf_op | source)
XLA Modules:
  0.0 57.1 jit_solution(9810514169598963203)
XLA Ops:
  0.6 51.6 %shard_map.121 = (f32[8,16,400]{2,1,0:T(8,128)}, f32[8,16,400]{2,1,0:T(8,128)}, f32[16,1024]{1,0:T(8,128)}) custom-call(f32[8,16,400]{2,1,0:T(8,128)} %volt_hbm.1, f32[8,16,400]{2,1,0:T(8,128)} %curr_hbm.1, bf16[8,400,400]{2,1,0:T(8,128)(2,1)} %linv_hbm.1, bf16[1024,512]{1,0:T(8,128)(2,1)} %schur_hbm.1, f32[8,400]{1,0:T(8,128)} %gain_hbm.1, ...), custom_call_target="tpu_custom_call" | custom-call | tf_op jit(solution)/shard_map/pallas_call | solution.py:346
  52.2 1.7 %copy.16 = f32[8,16,400]{2,1,0:T(8,128)} copy(f32[8,16,400]{2,1,0:T(8,128)} %get-tuple-element.6) | data formatting | bytes 409600
  53.9 1.7 %copy.17 = f32[8,16,400]{2,1,0:T(8,128)} copy(f32[8,16,400]{2,1,0:T(8,128)} %get-tuple-element.7) | data formatting | bytes 409600
  55.6 1.5 %copy.18 = f32[16,1024]{1,0:T(8,128)} copy(f32[16,1024]{1,0:T(8,128)} %get-tuple-element.8) | data formatting | bytes 131072

commit v3 on v2

--- a/solution.py
+++ b/solution.py
@@ -83,7 +83,6 @@
     piece = own_i // PIECES
     r = lax.axis_index("row")
     c = lax.axis_index("col")
-    others = rows * cols - 1
 
     loads = [
         pltpu.make_async_copy(src, dst, load_sem.at[n])
@@ -107,12 +106,10 @@
 
     barrier = pltpu.get_barrier_semaphore()
 
-    def greet(t, _):
-        there = (lax.rem(r + t // cols, rows), lax.rem(c + lax.rem(t, cols), cols))
+    friends = [(lax.rem(r + d, rows), c) for d in range(1, rows)]
+    friends += [(r, lax.rem(c + d, cols)) for d in range(1, cols)]
+    for there in friends:
         pl.semaphore_signal(barrier, inc=1, device_id=there, device_id_type=MESH)
-        return 0
-
-    lax.fori_loop(1, rows * cols, greet, 0)
     for load in loads[:-1]:
         load.wait()
 
@@ -180,7 +177,7 @@
                 )
 
     for step in range(STEPS):
-        base = 1 + (3 + PIECES) * step
+        base = 1 + (4 + PIECES) * step
         volt_now, curr_now = (volt_ref, curr_ref) if step == 0 else (volt_out, curr_out)
         injects = [injection(step, k, volt_now[k], curr_now[k]) for k in range(sub)]
         for k in range(sub):
@@ -198,7 +195,7 @@
         )
         val_in[step, r] = halves(vals)
         if step == 0:
-            pl.semaphore_wait(barrier, others)
+            pl.semaphore_wait(barrier, len(friends))
             for d in far_first:
                 send(map_ref, map_in.at[r], 0, (row_peer(d), c))
         for d in far_first:
@@ -225,19 +222,10 @@
         for b in range(cols):
             rhs_send[step, b] = rhs[:, b * share : (b + 1) * share]
 
-        def send_rhs(t, _):
-            peer_r = lax.rem(r + t // cols, rows)
-            peer_c = lax.rem(c + lax.rem(t, cols), cols)
-            send(
-                rhs_send.at[step, peer_c],
-                rhs_in.at[step, r * cols + c],
-                base + 1,
-                (peer_r, peer_c),
-            )
-            return 0
-
-        lax.fori_loop(1, rows * cols, send_rhs, 0)
-        rhs_in[step, r * cols + c] = rhs_send[step, c]
+        for d in range(1, cols):
+            peer = lax.rem(c + d, cols)
+            send(rhs_send.at[step, peer], rhs_in.at[step, r, c], base + 1, (r, peer))
+        rhs_in[step, r, c] = rhs_send[step, c]
 
         if step == 0:
 
@@ -248,13 +236,13 @@
             lax.fori_loop(1, rows, fill_rest_pick, 0)
             loads[-1].wait()
 
-        wait_bytes(rhs_in.at[step, pl.ds(0, others)], recv_sem.at[base + 1])
+        wait_bytes(rhs_in.at[step, r, pl.ds(0, cols - 1)], recv_sem.at[base + 1])
+        for d in far_first:
+            mine = rhs_in.at[step, r]
+            send(mine, mine, base + 2, (row_peer(d), c))
+        wait_bytes(rhs_in.at[step, pl.ds(0, rows - 1)], recv_sem.at[base + 2])
         wide = jnp.concatenate(
-            [
-                rhs_in[step, q * cols : (q + 1) * cols].reshape(cols * scen, share)
-                for q in range(rows)
-            ],
-            axis=1,
+            [rhs_in[step, q].reshape(cols * scen, share) for q in range(rows)], axis=1
         )
         for h in range(PIECES):
             part = dot_nt(wide, schur[h * piece : (h + 1) * piece, :]).astype(BF16)
@@ -264,13 +252,13 @@
                 send(
                     part_send.at[step, h, peer],
                     part_in.at[step, h, c],
-                    base + 2 + h,
+                    base + 3 + h,
                     (r, peer),
                 )
             part_in[step, h, c] = part_send[step, h, c]
 
         def summed(h):
-            wait_bytes(part_in.at[step, h, pl.ds(0, cols - 1)], recv_sem.at[base + 2 + h])
+            wait_bytes(part_in.at[step, h, pl.ds(0, cols - 1)], recv_sem.at[base + 3 + h])
             iface = part_in[step, h, 0].astype(F32)
             for b in range(1, cols):
                 iface += part_in[step, h, b].astype(F32)
@@ -294,10 +282,10 @@
                         send(
                             pick_send.at[step, q],
                             pick_in.at[step, r],
-                            base + 2 + PIECES,
+                            base + 3 + PIECES,
                             (q, c),
                         )
-        wait_bytes(pick_in.at[step, pl.ds(0, rows - 1)], recv_sem.at[base + 2 + PIECES])
+        wait_bytes(pick_in.at[step, pl.ds(0, rows - 1)], recv_sem.at[base + 3 + PIECES])
         picked = joined(pick_in[step, 0], scen)
         for q in range(1, rows):
             picked += joined(pick_in[step, q], scen)
@@ -315,12 +303,13 @@
 
     wait_bytes(map_in.at[pl.ds(0, rows - 1)], send_sem.at[0])
     for step in range(STEPS):
-        base = 1 + (3 + PIECES) * step
+        base = 1 + (4 + PIECES) * step
         wait_bytes(val_in.at[step, pl.ds(0, rows - 1)], send_sem.at[base])
-        wait_bytes(rhs_in.at[step, pl.ds(0, others)], send_sem.at[base + 1])
+        wait_bytes(rhs_in.at[step, 0, pl.ds(0, cols - 1)], send_sem.at[base + 1])
+        wait_bytes(rhs_in.at[step, pl.ds(0, rows - 1)], send_sem.at[base + 2])
         for h in range(PIECES):
-            wait_bytes(part_in.at[step, h, pl.ds(0, cols - 1)], send_sem.at[base + 2 + h])
-        wait_bytes(pick_in.at[step, pl.ds(0, rows - 1)], send_sem.at[base + 2 + PIECES])
+            wait_bytes(part_in.at[step, h, pl.ds(0, cols - 1)], send_sem.at[base + 3 + h])
+        wait_bytes(pick_in.at[step, pl.ds(0, rows - 1)], send_sem.at[base + 3 + PIECES])
 
 
 def fused(
@@ -369,14 +358,14 @@
             pltpu.VMEM((rows, own_i, flat), BF16),
             pltpu.VMEM((STEPS, rows, 2 * scen, flat), BF16),
             pltpu.VMEM((STEPS, cols, scen, share), BF16),
-            pltpu.VMEM((STEPS, rows * cols, scen, share), BF16),
+            pltpu.VMEM((STEPS, rows, cols, scen, share), BF16),
             pltpu.VMEM((STEPS, PIECES, cols, scen, own_i // PIECES), BF16),
             pltpu.VMEM((STEPS, PIECES, cols, scen, own_i // PIECES), BF16),
             pltpu.VMEM((STEPS, rows, 2 * scen, flat), BF16),
             pltpu.VMEM((STEPS, rows, 2 * scen, flat), BF16),
             pltpu.SemaphoreType.DMA((10,)),
-            pltpu.SemaphoreType.DMA((1 + (3 + PIECES) * STEPS,)),
-            pltpu.SemaphoreType.DMA((1 + (3 + PIECES) * STEPS,)),
+            pltpu.SemaphoreType.DMA((1 + (4 + PIECES) * STEPS,)),
+            pltpu.SemaphoreType.DMA((1 + (4 + PIECES) * STEPS,)),
             pltpu.SemaphoreType.DMA((STEPS, rows - 1)),
         ],
         compiler_params=pltpu.CompilerParams(

time: 57.3 us -> 59.2 us (1.033)
  Pallas kernels: 51.6 us -> 53.5 us
    pallas_call x1, Pallas kernels: 51.6 us -> 53.5 us  [fused(): pl.pallas_call(functools.partial(kernel, rows, cols), out_shape=(jax.Shap...]
where the time goes in v3:
time: 59.2 us; the launch traced here: 59 us
  Pallas kernels  53.5 us (90%)
  local copies, waits for them, and re-layouts  4.81 us (8%)
  between operations  0.64 us (1%)
    pallas_call x1, Pallas kernels, fused(): pl.pallas_call(functools.partial(kernel, rows, cols), out_shape=(jax.Shap...  53.5 us
    unnamed x3, local copies, waits for them, and re-layouts  4.81 us

profile of v3, /device:TPU:0, one launch (start us, length us, event | category | flops | bytes accessed | tf_op | source)
XLA Modules:
  0.0 59.0 jit_solution(6761424610040013819)
XLA Ops:
  0.6 53.5 %shard_map.121 = (f32[8,16,400]{2,1,0:T(8,128)}, f32[8,16,400]{2,1,0:T(8,128)}, f32[16,1024]{1,0:T(8,128)}) custom-call(f32[8,16,400]{2,1,0:T(8,128)} %volt_hbm.1, f32[8,16,400]{2,1,0:T(8,128)} %curr_hbm.1, bf16[8,400,400]{2,1,0:T(8,128)(2,1)} %linv_hbm.1, bf16[1024,512]{1,0:T(8,128)(2,1)} %schur_hbm.1, f32[8,400]{1,0:T(8,128)} %gain_hbm.1, ...), custom_call_target="tpu_custom_call" | custom-call | tf_op jit(solution)/shard_map/pallas_call | solution.py:335
  54.1 1.7 %copy.16 = f32[8,16,400]{2,1,0:T(8,128)} copy(f32[8,16,400]{2,1,0:T(8,128)} %get-tuple-element.6) | data formatting | bytes 409600
  55.8 1.7 %copy.17 = f32[8,16,400]{2,1,0:T(8,128)} copy(f32[8,16,400]{2,1,0:T(8,128)} %get-tuple-element.7) | data formatting | bytes 409600
  57.5 1.5 %copy.18 = f32[16,1024]{1,0:T(8,128)} copy(f32[16,1024]{1,0:T(8,128)} %get-tuple-element.8) | data formatting | bytes 131072

commit v4 on v2

--- a/solution.py
+++ b/solution.py
@@ -48,6 +48,8 @@
     node_hbm,
     volt_out,
     curr_out,
+    open_out,
+    picked_out,
     iface_out,
     volt_ref,
     curr_ref,
@@ -70,7 +72,10 @@
     part_in,
     pick_send,
     pick_in,
+    picked_ref,
+    iface_ref,
     load_sem,
+    store_sem,
     send_sem,
     recv_sem,
     val_sem,
@@ -179,10 +184,17 @@
                     m - e * LANES
                 )
 
+    stores = []
+
+    def store(src, dst):
+        copy = pltpu.make_async_copy(src, dst, store_sem.at[len(stores)])
+        copy.start()
+        stores.append(copy)
+
     for step in range(STEPS):
         base = 1 + (3 + PIECES) * step
-        volt_now, curr_now = (volt_ref, curr_ref) if step == 0 else (volt_out, curr_out)
-        injects = [injection(step, k, volt_now[k], curr_now[k]) for k in range(sub)]
+        last = step == STEPS - 1
+        injects = [injection(step, k, volt_ref[k], curr_ref[k]) for k in range(sub)]
         for k in range(sub):
             open_volt[k] = dot_nn(injects[k], linv[k])
 
@@ -197,6 +209,10 @@
             axis=1,
         )
         val_in[step, r] = halves(vals)
+        if last:
+            store(volt_ref, volt_out)
+            store(curr_ref, curr_out)
+            store(open_volt, open_out)
         if step == 0:
             pl.semaphore_wait(barrier, others)
             for d in far_first:
@@ -274,8 +290,8 @@
             iface = part_in[step, h, 0].astype(F32)
             for b in range(1, cols):
                 iface += part_in[step, h, b].astype(F32)
-            if step == STEPS - 1:
-                iface_out[:, h * piece : (h + 1) * piece] = iface
+            if last:
+                iface_ref[:, h * piece : (h + 1) * piece] = iface
             return halves(iface)
 
         order = far_first + [0]
@@ -297,22 +313,30 @@
                             base + 2 + PIECES,
                             (q, c),
                         )
+        if last:
+            store(iface_ref, iface_out)
         wait_bytes(pick_in.at[step, pl.ds(0, rows - 1)], recv_sem.at[base + 2 + PIECES])
         picked = joined(pick_in[step, 0], scen)
         for q in range(1, rows):
             picked += joined(pick_in[step, q], scen)
 
+        if last:
+            picked_ref[...] = picked
+            store(picked_ref, picked_out)
+            break
         drives = []
         for k in range(sub):
             first = (k % half) * LANES + (k // half) * ports
             drives.append((tie_ref[k : k + 1, :] * picked[:, first : first + ports]).astype(BF16))
         for k in range(sub):
-            volt, curr = volt_now[k], curr_now[k]
+            volt, curr = volt_ref[k], curr_ref[k]
             volt_next = open_volt[k] + dot_nn(drives[k], linv[k, :ports, :])
             closed = breaker_ref[k].astype(F32)
-            curr_out[k] = closed * (curr + gain_ref[k : k + 1, :] * (volt_next + volt))
-            volt_out[k] = volt_next
-
+            curr_ref[k] = closed * (curr + gain_ref[k : k + 1, :] * (volt_next + volt))
+            volt_ref[k] = volt_next
+
+    for copy in stores:
+        copy.wait()
     wait_bytes(map_in.at[pl.ds(0, rows - 1)], send_sem.at[0])
     for step in range(STEPS):
         base = 1 + (3 + PIECES) * step
@@ -321,6 +345,59 @@
         for h in range(PIECES):
             wait_bytes(part_in.at[step, h, pl.ds(0, cols - 1)], send_sem.at[base + 2 + h])
         wait_bytes(pick_in.at[step, pl.ds(0, rows - 1)], send_sem.at[base + 2 + PIECES])
+
+
+def update_kernel(
+    volt_hbm,
+    curr_hbm,
+    open_hbm,
+    linv_hbm,
+    gain_hbm,
+    tie_hbm,
+    breaker_hbm,
+    picked_hbm,
+    iface_hbm,
+    volt_out,
+    curr_out,
+    iface_out,
+    volt_ref,
+    curr_ref,
+    open_ref,
+    linv,
+    gain_ref,
+    tie_ref,
+    breaker_ref,
+    picked_ref,
+    load_sem,
+):
+    sub = volt_ref.shape[0]
+    ports = tie_ref.shape[1]
+    half = sub // 2
+    pairs = (
+        (linv_hbm.at[:, pl.ds(0, ports), :], linv),
+        (picked_hbm, picked_ref),
+        (tie_hbm, tie_ref),
+        (gain_hbm, gain_ref),
+        (open_hbm, open_ref),
+        (volt_hbm, volt_ref),
+        (curr_hbm, curr_ref),
+        (breaker_hbm, breaker_ref),
+        (iface_hbm, iface_out),
+    )
+    loads = [
+        pltpu.make_async_copy(src, dst, load_sem.at[n]) for n, (src, dst) in enumerate(pairs)
+    ]
+    for load in loads:
+        load.start()
+    for load in loads:
+        load.wait()
+    for k in range(sub):
+        first = (k % half) * LANES + (k // half) * ports
+        drive = (tie_ref[k : k + 1, :] * picked_ref[:, first : first + ports]).astype(BF16)
+        volt_next = open_ref[k] + dot_nn(drive, linv[k])
+        closed = breaker_ref[k].astype(F32)
+        curr_out[k] = closed * (curr_ref[k] + gain_ref[k : k + 1, :] * (volt_next + volt_ref[k]))
+        volt_out[k] = volt_next
 
 
 def fused(
@@ -343,15 +420,19 @@
     flat = sub * ports
     vmem = pl.BlockSpec(memory_space=pltpu.VMEM)
     hbm = pl.BlockSpec(memory_space=pltpu.HBM)
-    return pl.pallas_call(
+    state = jax.ShapeDtypeStruct(volt_init.shape, F32)
+    iface_shape = jax.ShapeDtypeStruct((scen, own_i), F32)
+    volt, curr, open_volt, picked, iface = pl.pallas_call(
         functools.partial(kernel, rows, cols),
         out_shape=(
-            jax.ShapeDtypeStruct(volt_init.shape, F32),
-            jax.ShapeDtypeStruct(volt_init.shape, F32),
-            jax.ShapeDtypeStruct((scen, own_i), F32),
+            state,
+            state,
+            state,
+            jax.ShapeDtypeStruct((scen, flat), F32),
+            iface_shape,
         ),
         in_specs=[hbm] * 10,
-        out_specs=(vmem, vmem, vmem),
+        out_specs=(hbm,) * 5,
         scratch_shapes=[
             pltpu.VMEM(volt_init.shape, F32),
             pltpu.VMEM(volt_init.shape, F32),
@@ -374,7 +455,10 @@
             pltpu.VMEM((STEPS, PIECES, cols, scen, own_i // PIECES), BF16),
             pltpu.VMEM((STEPS, rows, 2 * scen, flat), BF16),
             pltpu.VMEM((STEPS, rows, 2 * scen, flat), BF16),
+            pltpu.VMEM((scen, flat), F32),
+            pltpu.VMEM((scen, own_i), F32),
             pltpu.SemaphoreType.DMA((10,)),
+            pltpu.SemaphoreType.DMA((5,)),
             pltpu.SemaphoreType.DMA((1 + (3 + PIECES) * STEPS,)),
             pltpu.SemaphoreType.DMA((1 + (3 + PIECES) * STEPS,)),
             pltpu.SemaphoreType.DMA((STEPS, rows - 1)),
@@ -394,6 +478,24 @@
         fault_time,
         fault_node,
     )
+    return pl.pallas_call(
+        update_kernel,
+        out_shape=(state, state, iface_shape),
+        in_specs=[hbm] * 9,
+        out_specs=(vmem, vmem, vmem),
+        scratch_shapes=[
+            pltpu.VMEM(volt_init.shape, F32),
+            pltpu.VMEM(volt_init.shape, F32),
+            pltpu.VMEM(volt_init.shape, F32),
+            pltpu.VMEM((sub, ports, nodes), BF16),
+            pltpu.VMEM(ind_gain.shape, F32),
+            pltpu.VMEM(tie.shape, F32),
+            pltpu.VMEM(breaker.shape, jnp.int32),
+            pltpu.VMEM((scen, flat), F32),
+            pltpu.SemaphoreType.DMA((9,)),
+        ],
+        compiler_params=pltpu.CompilerParams(vmem_limit_bytes=60 * 1024 * 1024),
+    )(volt, curr, open_volt, local_inverse, ind_gain, tie, breaker, picked, iface)
 
 
 def plain(

time: 57.3 us -> 54.5 us (0.951)
  local copies, waits for them, and re-layouts: 4.81 us -> 0 us
  Pallas kernels: 51.6 us -> 53.7 us
    unnamed x3 -> x0, local copies, waits for them, and re-layouts: 4.81 us -> none
    pallas_call x1 -> x2, Pallas kernels: 51.6 us -> 53.7 us  [the longest x1 51.2 us: fused(): pl.pallas_call(functools.partial(kernel, rows, cols), out_shape=(state, s...]
where the time goes in v4:
time: 54.5 us; the launch traced here: 54.4 us
  Pallas kernels  53.7 us (99%)
  between operations  0.64 us (1%)
    pallas_call x1, Pallas kernels, fused(): pl.pallas_call(functools.partial(kernel, rows, cols), out_shape=(state, s...  51.2 us
    pallas_call x1, Pallas kernels, fused(): pl.pallas_call(update_kernel, out_shape=(state, state, iface_shape), in_s...  2.5 us

profile of v4, /device:TPU:0, one launch (start us, length us, event | category | flops | bytes accessed | tf_op | source)
XLA Modules:
  0.0 54.4 jit_solution(11261515958229405903)
XLA Ops:
  0.6 51.2 %shard_map.121 = (f32[8,16,400]{2,1,0:T(8,128)}, f32[8,16,400]{2,1,0:T(8,128)}, f32[8,16,400]{2,1,0:T(8,128)}, f32[16,512]{1,0:T(8,128)}, f32[16,1024]{1,0:T(8,128)}) custom-call(f32[8,16,400]{2,1,0:T(8,128)} %volt_hbm.1, f32[8,16,400]{2,1,0:T(8,128)} %curr_hbm.1, bf16[8,400,400]{2,1,0:T(8,128)(2,1)} %linv_hbm.3, bf16[1024,512]{1,0:T(8,128)(2,1)} %schur_hbm.1, ...), custom_call_target="tpu_custom_call" | custom-call | tf_op jit(solution)/shard_map/pallas_call | solution.py:425
  51.9 2.5 %shard_map.122 = (f32[8,16,400]{2,1,0:T(8,128)}, f32[8,16,400]{2,1,0:T(8,128)}, f32[16,1024]{1,0:T(8,128)}) custom-call(f32[8,16,400]{2,1,0:T(8,128)} %get-tuple-element.8.volt_hbm, f32[8,16,400]{2,1,0:T(8,128)} %get-tuple-element.9.curr_hbm, f32[8,16,400]{2,1,0:T(8,128)} %get-tuple-element.10.open_hbm, bf16[8,400,400]{2,1,0:T(8,128)(2,1)} %linv_hbm.3, ...), custom_call_target="tpu_custom_call" | custom-call | tf_op jit(solution)/shard_map/pallas_call | solution.py:481

commit v5 on v4

--- a/solution.py
+++ b/solution.py
@@ -112,12 +112,19 @@
 
     barrier = pltpu.get_barrier_semaphore()
 
-    def greet(t, _):
-        there = (lax.rem(r + t // cols, rows), lax.rem(c + lax.rem(t, cols), cols))
-        pl.semaphore_signal(barrier, inc=1, device_id=there, device_id_type=MESH)
-        return 0
-
-    lax.fori_loop(1, rows * cols, greet, 0)
+    row_peers = [r] + [lax.rem(r + d, rows) for d in range(1, rows)]
+    col_peers = [c] + [lax.rem(c + d, cols) for d in range(1, cols)]
+    far_rows = sorted(range(1, rows), key=lambda d: abs(d - rows // 2))
+    far_cols = sorted(range(1, cols), key=lambda d: abs(d - cols // 2))
+    for e in far_cols + [0]:
+        for d in far_rows + [0]:
+            if d or e:
+                pl.semaphore_signal(
+                    barrier,
+                    inc=1,
+                    device_id=(row_peers[d], col_peers[e]),
+                    device_id_type=MESH,
+                )
     for load in loads[:-1]:
         load.wait()
 
@@ -133,11 +140,6 @@
             device_id=there,
             device_id_type=MESH,
         ).start()
-
-    def row_peer(d):
-        return lax.rem(r + d, rows)
-
-    far_first = sorted(range(1, rows), key=lambda d: abs(d - rows // 2))
 
     scen_ids = lax.broadcasted_iota(jnp.int32, (scen, 1), 0)
     f_node = jnp.zeros((scen, 1), jnp.int32)
@@ -215,50 +217,50 @@
             store(open_volt, open_out)
         if step == 0:
             pl.semaphore_wait(barrier, others)
-            for d in far_first:
-                send(map_ref, map_in.at[r], 0, (row_peer(d), c))
-        for d in far_first:
+            for d in far_rows:
+                send(map_ref, map_in.at[r], 0, (row_peers[d], c))
+        for d in far_rows:
             mine = val_in.at[step, r]
-            send(mine, mine, base, (row_peer(d), c), val_sem.at[step, d - 1])
+            send(mine, mine, base, (row_peers[d], c), val_sem.at[step, d - 1])
 
         if step == 0:
             fill_spread(r, map_ref[...])
-            fill_pick(r, map_ref[...])
             wait_bytes(map_in.at[pl.ds(0, rows - 1)], recv_sem.at[0])
 
             def fill_rest(d, _):
-                fill_spread(row_peer(d), map_in[row_peer(d)])
+                q = lax.rem(r + d, rows)
+                fill_spread(q, map_in[q])
                 return 0
 
             lax.fori_loop(1, rows, fill_rest, 0)
 
         rhs = dot_nt(val_in[step, r], spread[r])
-        for d in reversed(far_first):
-            q = row_peer(rows - d)
+        for d in reversed(far_rows):
+            q = row_peers[rows - d]
             wait_bytes(val_in.at[step, q], val_sem.at[step, d - 1])
             rhs += dot_nt(val_in[step, q], spread[q])
         rhs = joined(rhs, scen).astype(BF16)
         for b in range(cols):
             rhs_send[step, b] = rhs[:, b * share : (b + 1) * share]
 
-        def send_rhs(t, _):
-            peer_r = lax.rem(r + t // cols, rows)
-            peer_c = lax.rem(c + lax.rem(t, cols), cols)
-            send(
-                rhs_send.at[step, peer_c],
-                rhs_in.at[step, r * cols + c],
-                base + 1,
-                (peer_r, peer_c),
-            )
-            return 0
-
-        lax.fori_loop(1, rows * cols, send_rhs, 0)
+        for e in far_cols + [0]:
+            for d in far_rows + [0]:
+                if d or e:
+                    send(
+                        rhs_send.at[step, col_peers[e]],
+                        rhs_in.at[step, r * cols + c],
+                        base + 1,
+                        (row_peers[d], col_peers[e]),
+                    )
         rhs_in[step, r * cols + c] = rhs_send[step, c]
 
         if step == 0:
 
+            fill_pick(r, map_ref[...])
+
             def fill_rest_pick(d, _):
-                fill_pick(row_peer(d), map_in[row_peer(d)])
+                q = lax.rem(r + d, rows)
+                fill_pick(q, map_in[q])
                 return 0
 
             lax.fori_loop(1, rows, fill_rest_pick, 0)
@@ -275,8 +277,8 @@
         for h in range(PIECES):
             part = dot_nt(wide, schur[h * piece : (h + 1) * piece, :]).astype(BF16)
             part_send[step, h] = part.reshape(cols, scen, piece)
-            for d in range(1, cols):
-                peer = lax.rem(c + d, cols)
+            for e in far_cols:
+                peer = col_peers[e]
                 send(
                     part_send.at[step, h, peer],
                     part_in.at[step, h, c],
@@ -294,12 +296,12 @@
                 iface_ref[:, h * piece : (h + 1) * piece] = iface
             return halves(iface)
 
-        order = far_first + [0]
+        order = far_rows + [0]
         totals = {}
         for h in range(PIECES):
             iface = summed(h)
             for d in order:
-                q = row_peer(d)
+                q = row_peers[d]
                 term = dot_nn(iface, pick[q, h * piece : (h + 1) * piece, :])
                 totals[d] = term if h == 0 else totals[d] + term
                 if h == PIECES - 1:

time: 54.5 us -> 55.2 us (1.013)
  Pallas kernels: 53.7 us -> 54.4 us
    pallas_call x1, Pallas kernels: 51.2 us -> 51.9 us  [fused(): pl.pallas_call(functools.partial(kernel, rows, cols), out_shape=(state, s...]
where the time goes in v5:
time: 55.2 us; the launch traced here: 55 us
  Pallas kernels  54.4 us (99%)
  between operations  0.64 us (1%)
    pallas_call x1, Pallas kernels, fused(): pl.pallas_call(functools.partial(kernel, rows, cols), out_shape=(state, s...  51.9 us
    pallas_call x1, Pallas kernels, fused(): pl.pallas_call(update_kernel, out_shape=(state, state, iface_shape), in_s...  2.5 us

profile of v5, /device:TPU:0, one launch (start us, length us, event | category | flops | bytes accessed | tf_op | source)
XLA Modules:
  0.0 55.0 jit_solution(18303083677242079439)
XLA Ops:
  0.6 51.9 %shard_map.121 = (f32[8,16,400]{2,1,0:T(8,128)}, f32[8,16,400]{2,1,0:T(8,128)}, f32[8,16,400]{2,1,0:T(8,128)}, f32[16,512]{1,0:T(8,128)}, f32[16,1024]{1,0:T(8,128)}) custom-call(f32[8,16,400]{2,1,0:T(8,128)} %volt_hbm.1, f32[8,16,400]{2,1,0:T(8,128)} %curr_hbm.1, bf16[8,400,400]{2,1,0:T(8,128)(2,1)} %linv_hbm.3, bf16[1024,512]{1,0:T(8,128)(2,1)} %schur_hbm.1, ...), custom_call_target="tpu_custom_call" | custom-call | tf_op jit(solution)/shard_map/pallas_call | solution.py:427
  52.5 2.5 %shard_map.122 = (f32[8,16,400]{2,1,0:T(8,128)}, f32[8,16,400]{2,1,0:T(8,128)}, f32[16,1024]{1,0:T(8,128)}) custom-call(f32[8,16,400]{2,1,0:T(8,128)} %get-tuple-element.8.volt_hbm, f32[8,16,400]{2,1,0:T(8,128)} %get-tuple-element.9.curr_hbm, f32[8,16,400]{2,1,0:T(8,128)} %get-tuple-element.10.open_hbm, bf16[8,400,400]{2,1,0:T(8,128)(2,1)} %linv_hbm.3, ...), custom_call_target="tpu_custom_call" | custom-call | tf_op jit(solution)/shard_map/pallas_call | solution.py:483

commit v6 on v4

--- a/solution.py
+++ b/solution.py
@@ -55,6 +55,7 @@
     curr_ref,
     linv,
     schur,
+    turned,
     gain_ref,
     tie_ref,
     map_ref,
@@ -156,6 +157,7 @@
         return (-hist - 2.0 * fault_on * volt).astype(BF16)
 
     ids = lax.broadcasted_iota(jnp.int32, (LANES, LANES), 0).astype(F32).astype(BF16)
+    lane_ids = lax.broadcasted_iota(jnp.int32, (1, LANES), 1)
     one = jnp.ones((LANES, LANES), BF16)
     zero = jnp.zeros((LANES, LANES), BF16)
 
@@ -168,13 +170,15 @@
 
     def fill_spread(q, maps):
         for g in range(half):
-            m = packed_map(maps, g)
+            m = packed_map(maps, g).astype(F32)
+            down = jnp.broadcast_to(m, (LANES, LANES)).T
             for b in range(cols):
                 for e in range(share // LANES):
                     first = b * share + e * LANES
-                    spread[q, first : first + LANES, g * LANES : (g + 1) * LANES] = hits(
-                        m - (b * own_j + r * share + e * LANES)
-                    )
+                    across = lane_ids + (b * own_j + r * share + e * LANES)
+                    spread[q, g * LANES : (g + 1) * LANES, first : first + LANES] = jnp.where(
+                        down == across.astype(F32), 1.0, 0.0
+                    ).astype(BF16)
 
     def fill_pick(q, maps):
         for g in range(half):
@@ -232,11 +236,11 @@
 
             lax.fori_loop(1, rows, fill_rest, 0)
 
-        rhs = dot_nt(val_in[step, r], spread[r])
+        rhs = dot_nn(val_in[step, r], spread[r])
         for d in reversed(far_first):
             q = row_peer(rows - d)
             wait_bytes(val_in.at[step, q], val_sem.at[step, d - 1])
-            rhs += dot_nt(val_in[step, q], spread[q])
+            rhs += dot_nn(val_in[step, q], spread[q])
         rhs = joined(rhs, scen).astype(BF16)
         for b in range(cols):
             rhs_send[step, b] = rhs[:, b * share : (b + 1) * share]
@@ -263,6 +267,7 @@
 
             lax.fori_loop(1, rows, fill_rest_pick, 0)
             loads[-1].wait()
+            turned[...] = schur[...].T
 
         wait_bytes(rhs_in.at[step, pl.ds(0, others)], recv_sem.at[base + 1])
         wide = jnp.concatenate(
@@ -273,7 +278,7 @@
             axis=1,
         )
         for h in range(PIECES):
-            part = dot_nt(wide, schur[h * piece : (h + 1) * piece, :]).astype(BF16)
+            part = dot_nn(wide, turned[:, h * piece : (h + 1) * piece]).astype(BF16)
             part_send[step, h] = part.reshape(cols, scen, piece)
             for d in range(1, cols):
                 peer = lax.rem(c + d, cols)
@@ -438,6 +443,7 @@
             pltpu.VMEM(volt_init.shape, F32),
             pltpu.VMEM(local_inverse.shape, BF16),
             pltpu.VMEM(schur_inverse.shape, BF16),
+            pltpu.VMEM((own_j, own_i), BF16),
             pltpu.VMEM(ind_gain.shape, F32),
             pltpu.VMEM(tie.shape, F32),
             pltpu.VMEM(port_map.shape, jnp.int32),
@@ -446,7 +452,7 @@
             pltpu.SMEM(fault_node.shape, jnp.int32),
             pltpu.VMEM(volt_init.shape, F32),
             pltpu.VMEM((rows, sub, ports), jnp.int32),
-            pltpu.VMEM((rows, cols * share, flat), BF16),
+            pltpu.VMEM((rows, flat, cols * share), BF16),
             pltpu.VMEM((rows, own_i, flat), BF16),
             pltpu.VMEM((STEPS, rows, 2 * scen, flat), BF16),
             pltpu.VMEM((STEPS, cols, scen, share), BF16),

time: 54.5 us -> 53.7 us (0.985)
  Pallas kernels: 53.7 us -> 52.9 us
    pallas_call x1, Pallas kernels: 51.2 us -> 50.4 us  [fused(): pl.pallas_call(functools.partial(kernel, rows, cols), out_shape=(state, s...]
where the time goes in v6:
time: 53.7 us; the launch traced here: 53.6 us
  Pallas kernels  52.9 us (99%)
  between operations  0.64 us (1%)
    pallas_call x1, Pallas kernels, fused(): pl.pallas_call(functools.partial(kernel, rows, cols), out_shape=(state, s...  50.4 us
    pallas_call x1, Pallas kernels, fused(): pl.pallas_call(update_kernel, out_shape=(state, state, iface_shape), in_s...  2.5 us

profile of v6, /device:TPU:0, one launch (start us, length us, event | category | flops | bytes accessed | tf_op | source)
XLA Modules:
  0.0 53.6 jit_solution(4606762420632573800)
XLA Ops:
  0.6 50.4 %shard_map.121 = (f32[8,16,400]{2,1,0:T(8,128)}, f32[8,16,400]{2,1,0:T(8,128)}, f32[8,16,400]{2,1,0:T(8,128)}, f32[16,512]{1,0:T(8,128)}, f32[16,1024]{1,0:T(8,128)}) custom-call(f32[8,16,400]{2,1,0:T(8,128)} %volt_hbm.1, f32[8,16,400]{2,1,0:T(8,128)} %curr_hbm.1, bf16[8,400,400]{2,1,0:T(8,128)(2,1)} %linv_hbm.3, bf16[1024,512]{1,0:T(8,128)(2,1)} %schur_hbm.1, ...), custom_call_target="tpu_custom_call" | custom-call | tf_op jit(solution)/shard_map/pallas_call | solution.py:430
  51.1 2.5 %shard_map.122 = (f32[8,16,400]{2,1,0:T(8,128)}, f32[8,16,400]{2,1,0:T(8,128)}, f32[16,1024]{1,0:T(8,128)}) custom-call(f32[8,16,400]{2,1,0:T(8,128)} %get-tuple-element.8.volt_hbm, f32[8,16,400]{2,1,0:T(8,128)} %get-tuple-element.9.curr_hbm, f32[8,16,400]{2,1,0:T(8,128)} %get-tuple-element.10.open_hbm, bf16[8,400,400]{2,1,0:T(8,128)(2,1)} %linv_hbm.3, ...), custom_call_target="tpu_custom_call" | custom-call | tf_op jit(solution)/shard_map/pallas_call | solution.py:487

commit v7 on v6

--- a/solution.py
+++ b/solution.py
@@ -8,7 +8,7 @@
 from jax.sharding import PartitionSpec as P
 
 STEPS = 2
-PIECES = 2
+PIECES = 1
 LANES = 128
 MESH = pl.DeviceIdType.MESH
 F32 = jnp.float32

time: 53.7 us -> 52.2 us (0.972)
  Pallas kernels: 52.9 us -> 51.4 us
    pallas_call x1, Pallas kernels: 50.4 us -> 48.9 us  [fused(): pl.pallas_call(functools.partial(kernel, rows, cols), out_shape=(state, s...]
where the time goes in v7:
time: 52.2 us; the launch traced here: 52 us
  Pallas kernels  51.4 us (98%)
  between operations  0.64 us (1%)
    pallas_call x1, Pallas kernels, fused(): pl.pallas_call(functools.partial(kernel, rows, cols), out_shape=(state, s...  48.9 us
    pallas_call x1, Pallas kernels, fused(): pl.pallas_call(update_kernel, out_shape=(state, state, iface_shape), in_s...  2.5 us

profile of v7, /device:TPU:0, one launch (start us, length us, event | category | flops | bytes accessed | tf_op | source)
XLA Modules:
  0.0 52.0 jit_solution(17514605058091406617)
XLA Ops:
  0.6 48.9 %shard_map.121 = (f32[8,16,400]{2,1,0:T(8,128)}, f32[8,16,400]{2,1,0:T(8,128)}, f32[8,16,400]{2,1,0:T(8,128)}, f32[16,512]{1,0:T(8,128)}, f32[16,1024]{1,0:T(8,128)}) custom-call(f32[8,16,400]{2,1,0:T(8,128)} %volt_hbm.1, f32[8,16,400]{2,1,0:T(8,128)} %curr_hbm.1, bf16[8,400,400]{2,1,0:T(8,128)(2,1)} %linv_hbm.3, bf16[1024,512]{1,0:T(8,128)(2,1)} %schur_hbm.1, ...), custom_call_target="tpu_custom_call" | custom-call | tf_op jit(solution)/shard_map/pallas_call | solution.py:430
  49.5 2.5 %shard_map.122 = (f32[8,16,400]{2,1,0:T(8,128)}, f32[8,16,400]{2,1,0:T(8,128)}, f32[16,1024]{1,0:T(8,128)}) custom-call(f32[8,16,400]{2,1,0:T(8,128)} %get-tuple-element.8.volt_hbm, f32[8,16,400]{2,1,0:T(8,128)} %get-tuple-element.9.curr_hbm, f32[8,16,400]{2,1,0:T(8,128)} %get-tuple-element.10.open_hbm, bf16[8,400,400]{2,1,0:T(8,128)(2,1)} %linv_hbm.3, ...), custom_call_target="tpu_custom_call" | custom-call | tf_op jit(solution)/shard_map/pallas_call | solution.py:487
